TPU v7x, 512 devices: a whole 4x4x16 slice. The times are simulated.
512 devices in a mesh: dp: 32 (over z, x_hi), fsdp: 16 (over x_lo, y, core).
Axes of the slice: x: 4 (x_hi: 2, x_lo: 2; x = x_hi * 2 + x_lo), y: 4, z: 16, core: 2. Of those that a mesh axis runs over, the one named last changes fastest.
Arguments:
- layer_inputs: bfloat16 [65536, 4096], P(('dp', 'fsdp')), may hold values from -6 to 6
- output_grads: bfloat16 [65536, 12288], P(('dp', 'fsdp')), may hold values from -6 to 6
- slot_block_table: int32 [16], replicated, may hold values from 0 to 15, each once
- weight_gradient_pairs: bfloat16 [48, 1024, 1024], P('fsdp', 'dp'), may hold values from -6 to 6
- basis_in: bfloat16 [4, 1024, 1024], P(None, None, 'dp'), may hold values from -0.1875 to 0.1875
- basis_out: bfloat16 [12, 1024, 1024], P(None, 'dp', 'fsdp'), may hold values from -0.1875 to 0.1875
- values_in: float32 [4, 1024], replicated, may hold values from 0.3 to 3
- values_out: float32 [12, 1024], replicated, may hold values from 0.3 to 3
Outputs:
- covariance: float32 [16, 1024, 1024], P('fsdp', 'dp')
- preconditioned: bfloat16 [48, 1024, 1024], P('fsdp', 'dp')
Inputs may be any that keep to these rules, and one draw needn't show every extreme that they name: `slot_block_table`: each of the 16 factor blocks stands in exactly one slot.
All inputs are finite; a program needn't handle non-finite values.
Results may differ from a plain program's by a relative error of at most 0.017.
Values may be sent and summed in bfloat16 or wider, within the bound.
No kernel may reach another device: no remote copies, remote signals or barrier semaphores. Data moves between devices by JAX's collectives and lax.ppermute only.
A program may use at most 64 MiB of HBM per device.

v0:
```python
import jax
import jax.numpy as jnp
import numpy as np
from jax import lax
from jax.sharding import PartitionSpec as P

damping = 0.1


def body(
    layer_inputs,
    output_grads,
    slot_block_table,
    weight_gradient_pairs,
    basis_in,
    basis_out,
    values_in,
    values_out,
):
    tokens_dev = layer_inputs.shape[0]
    block_size = values_in.shape[1]
    count_in = layer_inputs.shape[1] // block_size
    count_out = output_grads.shape[1] // block_size
    count_slots = count_in + count_out
    fsdp_size = lax.axis_size("fsdp")
    dp_size = lax.axis_size("dp")
    pairs_dev = weight_gradient_pairs.shape[0]
    cols_dev = block_size // dp_size
    one_hot_selector = (
        slot_block_table[None, :] == jnp.arange(count_slots, dtype=jnp.int32)[:, None]
    ).astype(jnp.bfloat16)
    input_triple = layer_inputs.reshape(tokens_dev, count_in, block_size)
    grads_three = output_grads.reshape(tokens_dev, count_out, block_size)
    sorted_slots = (
        jnp.einsum(
            "tsb,su->tub",
            input_triple,
            one_hot_selector[:count_in],
            preferred_element_type=jnp.float32,
        )
        + jnp.einsum(
            "tsb,su->tub",
            grads_three,
            one_hot_selector[count_in:],
            preferred_element_type=jnp.float32,
        )
    ).astype(jnp.bfloat16)
    first_out = np.arange(fsdp_size) * pairs_dev % count_out
    wanted = (first_out[:, None] + np.arange(pairs_dev)[None, :]).reshape(-1)
    chosen = basis_out[wanted]
    outgoing = jnp.transpose(chosen, (2, 0, 1))
    gathered_tokens, basis_cols = (
        lax.all_to_all(sorted_slots, "fsdp", split_axis=1, concat_axis=0, tiled=True),
        lax.all_to_all(outgoing, "fsdp", split_axis=1, concat_axis=0, tiled=True),
    )
    total_tokens = tokens_dev * dp_size * fsdp_size
    partial_cov = jnp.einsum(
        "tsb,tsc->sbc", gathered_tokens, gathered_tokens, preferred_element_type=jnp.float32
    )
    covariance = (
        lax.psum_scatter(
            partial_cov.astype(jnp.bfloat16), "dp", scatter_dimension=1, tiled=True
        ).astype(jnp.float32)
        / total_tokens
    )
    position = lax.axis_index("fsdp") * pairs_dev
    block_left = position // count_out
    start_out = position % count_out
    left_piece = lax.dynamic_index_in_dim(basis_in, block_left, 0, keepdims=True)
    right_full, left_full = (
        lax.all_gather(basis_cols, "dp", axis=2, tiled=True),
        lax.all_gather(jnp.transpose(left_piece, (1, 0, 2)), "dp", axis=2, tiled=True),
    )
    basis_left = left_full[:, 0, :]
    rotated = jnp.einsum(
        "prc,dpc->prd", weight_gradient_pairs, right_full, preferred_element_type=jnp.float32
    ).astype(jnp.bfloat16)
    columns = lax.all_to_all(rotated, "dp", split_axis=2, concat_axis=1, tiled=True)
    inner_rot = jnp.einsum(
        "rk,prc->pkc", basis_left, columns, preferred_element_type=jnp.float32
    ).astype(jnp.bfloat16)
    col_start = lax.axis_index("dp") * cols_dev
    right_vals = lax.dynamic_slice_in_dim(values_out, start_out, pairs_dev, 0)
    right_vals = lax.dynamic_slice_in_dim(right_vals, col_start, cols_dev, 1)
    left_vals = lax.dynamic_index_in_dim(values_in, block_left, 0, keepdims=False)
    denom = left_vals[None, :, None] * right_vals[:, None, :] + damping
    scaled = (inner_rot.astype(jnp.float32) / denom).astype(jnp.bfloat16)
    back_rot = jnp.einsum(
        "rk,pkc->prc", basis_left, scaled, preferred_element_type=jnp.float32
    ).astype(jnp.bfloat16)
    rows_again = lax.all_to_all(back_rot, "dp", split_axis=1, concat_axis=2, tiled=True)
    preconditioned = jnp.einsum(
        "prd,dpc->prc", rows_again, right_full, preferred_element_type=jnp.float32
    ).astype(jnp.bfloat16)
    return (covariance, preconditioned)


def solution(mesh):
    placed = (
        P(("dp", "fsdp"), None),
        P(("dp", "fsdp"), None),
        P(),
        P("fsdp", "dp", None),
        P(None, None, "dp"),
        P(None, "dp", "fsdp"),
        P(),
        P(),
    )
    return jax.shard_map(
        body,
        mesh=mesh,
        in_specs=placed,
        out_specs=(P("fsdp", "dp", None), P("fsdp", "dp", None)),
        check_vma=False,
    )
```

profile of v0, /device:TPU:8, one launch (start us, length us, event | category | flops | bytes accessed | tf_op | source)
XLA Modules:
  0.0 1015.2 jit_solution(12233313240462907014)
XLA Ops:
  7.2 0.0 copy-start
  7.2 0.0 all-gather.4.cloned.1.call-start
  7.2 0.8 pad_clamp_fusion
  8.0 1.5 gather_fusion
  9.5 0.2 reshape.41
  9.8 13.3 %all_to_all.69 = bf16[16,2,3072]{2,1,0:T(2,128)(2,1)S(1)} all-to-all(bf16[16,2,3072]{2,1,0:T(2,128)(2,1)S(1)} %reshape.41), channel_id=1, replica_groups=mesh['dp'=32,'fsdp'=16] {'fsdp'}, dimensions={0} | all-to-all | bytes 393216 | tf_op jit(solution)/shard_map/all_to_all | solution.py:54
  23.1 0.3 reshape.42
  23.4 0.2 copy.51
  23.6 1.0 all_to_all.56
  24.5 0.0 all-gather.4.cloned.1.call-update
  24.6 1.6 reshape.24
  26.1 3.5 copy.27
  29.6 0.0 copy-start.4
  29.6 7.0 copy.29
  36.6 2.7 fusion.44
  39.4 1.6 fusion
  41.0 4.4 copy.30
  45.3 6.7 all-to-all-start
  52.1 0.0 all-gather.6.cloned.1.call-start
  52.2 0.6 constant_dynamic-slice_fusion.1
  52.8 0.0 all-gather.6.cloned.1.call-update
  52.8 0.0 copy-start.3
  52.8 0.2 reduce-scatter.2.cloned.1.call-start
  53.1 58.4 %all-to-all-done = bf16[128,16,1024]{2,0,1:T(8,128)(2,1)} async-done(((bf16[128,16,1024]{2,0,1:T(8,128)(2,1)}), bf16[128,16,1024]{2,0,1:T(8,128)(2,1)}, u32[]{:S(2)}, u32[]{:S(2)}) %all-to-all-start) | async-done | bytes 4194336 | tf_op jit(solution)/shard_map/all_to_all | solution.py:53
  111.5 13.2 %fusion.4 = bf16[1,1024,1024]{2,1,0:T(8,128)(2,1)} fusion(bf16[128,16,1024]{2,0,1:T(8,128)(2,1)} %all-to-all-done), kind=kOutput, calls=%fused_computation.7 | convolution fusion | flops 4296015872 | bytes 6291456 | tf_op jit(solution)/shard_map/tsb,tsc->sbc/dot_general | solution.py:57
  124.7 0.0 reduce-scatter.2.cloned.1.call-update
  124.7 80.0 %all-gather.4.cloned.1.call-done = bf16[1024,3,1024]{0,2,1:T(8,128)(2,1)} async-done(((bf16[1024,3,32]{0,2,1:T(8,128)(2,1)}), bf16[1024,3,1024]{0,2,1:T(8,128)(2,1)}) %all-gather.4.cloned.1.call-update) | async-done | bytes 6291472 | tf_op jit(solution)/shard_map/all_gather | solution.py:71
  204.6 4.0 fusion.38
  208.6 0.7 copy.33
  209.3 1.4 reshape.43
  210.7 8.2 all-to-all-start.2
  218.9 0.8 dynamic_slice.14
  219.7 0.7 constant_dynamic-slice_fusion
  220.4 15.4 %all-to-all-done.2 = bf16[32,2,1536]{2,1,0:T(2,128)(2,1)S(1)} async-done(((bf16[32,2,1536]{2,1,0:T(2,128)(2,1)}), bf16[32,2,1536]{2,1,0:T(2,128)(2,1)S(1)}, u32[]{:S(2)}, u32[]{:S(2)}) %all-to-all-start.2) | async-done | bytes 196640 | tf_op jit(solution)/shard_map/all_to_all | solution.py:78
  235.8 0.7 reshape.44
  236.5 0.6 copy.50
  237.2 0.8 all_to_all.60
  238.0 115.4 %all-gather.6.cloned.1.call-done = bf16[1,1024,1024]{1,2,0:T(8,128)(2,1)} async-done(((bf16[1,1024,32]{1,2,0:T(8,128)(2,1)}), bf16[1,1024,1024]{1,2,0:T(8,128)(2,1)}) %all-gather.6.cloned.1.call-update) | async-done | bytes 2097168 | tf_op jit(solution)/shard_map/all_gather | solution.py:72
  353.4 3.3 fusion.33
  356.8 0.7 copy.36
  357.5 1.4 reshape.45
  358.9 7.4 all-to-all-start.3
  366.3 633.3 %reduce-scatter.2.cloned.1.call-done = bf16[1,32,1024]{2,1,0:T(8,128)(2,1)} async-done(((bf16[1,1024,1024]{2,1,0:T(8,128)(2,1)}), bf16[1,32,1024]{2,1,0:T(8,128)(2,1)}) %reduce-scatter.2.cloned.1.call-update) | async-done | bytes 65552 | tf_op jit(solution)/shard_map/reduce_scatter | solution.py:61
  999.6 1.5 convert_multiply_fusion
  1001.1 0.7 reshape.46
  1001.8 0.6 copy.49
  1002.4 0.8 all_to_all.64
  1003.2 5.4 convolution_convert_fusion.1
  (10 shorter events, 0.1 us)
Async XLA Ops:
  7.2 45.0 %copy-start = (bf16[4,1024,32]{1,2,0:T(8,128)(2,1)S(1)}, bf16[4,1024,32]{1,2,0:T(8,128)(2,1)}, u32[]{:S(2)}) copy-start(bf16[4,1024,32]{1,2,0:T(8,128)(2,1)} %param.14) | copy-start | bytes 786436
  7.2 17.4 %copy-start.2 = (bf16[128,4096]{1,0:T(8,128)(2,1)S(1)}, bf16[128,4096]{1,0:T(8,128)(2,1)}, u32[]{:S(2)}) copy-start(bf16[128,4096]{1,0:T(8,128)(2,1)} %param.10) | copy-start | bytes 3145732
  7.2 197.4 %all-gather.4.cloned.1.call-start = ((), (), s32[]{:S(2)}) async-start(), calls=%async_computation.6 | async-start | bytes 6488064 | tf_op jit(solution)/shard_map/all_gather | solution.py:71
  29.6 7.0 copy-start.4
  36.6 2.7 copy-start.1
  45.3 66.1 %all-to-all-start = ((bf16[128,16,1024]{2,0,1:T(8,128)(2,1)}), bf16[128,16,1024]{2,0,1:T(8,128)(2,1)}, u32[]{:S(2)}, u32[]{:S(2)}) async-start(bf16[128,16,1024]{2,0,1:T(8,128)(2,1)} %copy.30), calls=%async_computation | async-start | bytes 8388608 | tf_op jit(solution)/shard_map/all_to_all | solution.py:53
  52.1 301.3 %all-gather.6.cloned.1.call-start = ((), (), s32[]{:S(2)}) async-start(), calls=%async_computation.7 | async-start | bytes 2162688 | tf_op jit(solution)/shard_map/all_gather | solution.py:72
  52.8 151.8 %copy-start.3 = (bf16[3,32,1024]{2,1,0:T(8,128)(2,1)S(1)}, bf16[3,32,1024]{2,1,0:T(8,128)(2,1)}, u32[]{:S(2)}) copy-start(bf16[3,32,1024]{2,1,0:T(8,128)(2,1)} %param.13) | copy-start | bytes 589828
  52.8 946.7 %reduce-scatter.2.cloned.1.call-start = ((), (), s32[]{:S(2)}) async-start(), calls=%async_computation.5 | async-start | bytes 2162688 | tf_op jit(solution)/shard_map/reduce_scatter | solution.py:61
  210.7 25.1 %all-to-all-start.2 = ((bf16[32,2,1536]{2,1,0:T(2,128)(2,1)}), bf16[32,2,1536]{2,1,0:T(2,128)(2,1)S(1)}, u32[]{:S(2)}, u32[]{:S(2)}) async-start(bf16[32,2,1536]{2,1,0:T(2,128)(2,1)} %reshape.43), calls=%async_computation.3 | async-start | bytes 393216 | tf_op jit(solution)/shard_map/all_to_all | solution.py:78
  358.9 642.2 %all-to-all-start.3 = ((bf16[32,2,1536]{2,1,0:T(2,128)(2,1)}), bf16[32,2,1536]{2,1,0:T(2,128)(2,1)S(1)}, u32[]{:S(2)}, u32[]{:S(2)}) async-start(bf16[32,2,1536]{2,1,0:T(2,128)(2,1)} %reshape.45), calls=%async_computation.4 | async-start | bytes 393216 | tf_op jit(solution)/shard_map/all_to_all | solution.py:91
Sparse Core Ops, SparseCore 0:
  24.7 179.9 all-gather.3
  208.3 145.0 all-gather.5
  357.8 641.7 reduce-scatter.1
where the time goes:
time: 1020 us
  waiting for transfers between devices  903 us (89%)
  local copies, waits for them, and re-layouts  30.3 us (3%)
  matrix products  30.2 us (3%)
  starting transfers between devices  22.6 us (2%)
  between operations  14 us (1%)
  blocking collectives  13.3 us (1%)
    reduce_scatter x1, waiting for transfers between devices, body(): lax.psum_scatter(partial_cov.astype(jnp.bfloat16), 'dp', scatter_dimensio...  633 us
    all_gather x1, waiting for transfers between devices, body(): lax.all_gather(jnp.transpose(left_piece, (1, 0, 2)), 'dp', axis=2, tiled=...  115 us
    all_gather x1, waiting for transfers between devices, body(): lax.all_gather(basis_cols, 'dp', axis=2, tiled=True)  80 us
    all_to_all x1, waiting for transfers between devices, body(): lax.all_to_all(sorted_slots, 'fsdp', split_axis=1, concat_axis=0, tiled=T...  58.4 us
  transfers between devices with their start and end apart: 6, of which 5 were waited for; matrix products, arithmetic and copies ran while one was open for 5% of the time, Pallas kernels for 0%

commit v1 on v0

v1 whole, which is shorter than its diff:
```python
import jax
import jax.numpy as jnp
from jax import lax
from jax.experimental import pallas as pl
from jax.experimental.pallas import tpu as pltpu
from jax.sharding import Mesh, PartitionSpec as P

damping = 0.1
block = 1024
axes = ("z", "xh", "xl", "yh", "yl", "c")
sizes = (16, 2, 2, 2, 2, 2)
dp = ("z", "xh")
fsdp = ("xl", "yh", "yl", "c")
plane = ("xh", "xl", "yh", "yl", "c")
row_group = ("xh", "yl", "c")
col_group = ("xl", "yh")
n_dp = 32
n_fsdp = 16
rows = block // n_dp
mib = 1024 * 1024


def cost(flops, nbytes):
    return pl.CostEstimate(flops=flops, bytes_accessed=nbytes, transcendentals=0)


def in_vmem(count):
    return [pl.BlockSpec(memory_space=pltpu.VMEM)] * count


def nt(a, b):
    return lax.dot_general(a, b, (((1,), (1,)), ((), ())), preferred_element_type=jnp.float32)


def tn(a, b):
    return lax.dot_general(a, b, (((0,), (0,)), ((), ())), preferred_element_type=jnp.float32)


def sort_kernel(table, inputs, grads, out, sems):
    count_in = inputs.shape[1] // block
    for slot in range(out.shape[0]):
        b = table[slot]

        @pl.when(b < count_in)
        def _():
            start = pl.multiple_of(b * block, block)
            pltpu.make_async_copy(
                inputs.at[:, pl.ds(start, block)], out.at[slot], sems.at[slot]
            ).start()

        @pl.when(b >= count_in)
        def _():
            start = pl.multiple_of((b - count_in) * block, block)
            pltpu.make_async_copy(
                grads.at[:, pl.ds(start, block)], out.at[slot], sems.at[slot]
            ).start()

    for slot in range(out.shape[0]):
        pltpu.make_async_copy(
            inputs.at[:, pl.ds(0, block)], out.at[slot], sems.at[slot]
        ).wait()


def sort_slots(table, inputs, grads):
    tokens = inputs.shape[0]
    slots = (inputs.shape[1] + grads.shape[1]) // block
    return pl.pallas_call(
        sort_kernel,
        out_shape=jax.ShapeDtypeStruct((slots, tokens, block), inputs.dtype),
        in_specs=[
            pl.BlockSpec(memory_space=pltpu.SMEM),
            pl.BlockSpec(memory_space=pl.ANY),
            pl.BlockSpec(memory_space=pl.ANY),
        ],
        out_specs=pl.BlockSpec(memory_space=pltpu.VMEM),
        scratch_shapes=[pltpu.SemaphoreType.DMA((slots,))],
        compiler_params=pltpu.CompilerParams(vmem_limit_bytes=24 * mib),
        cost_estimate=cost(0, 4 * slots * tokens * block),
    )(table, inputs, grads)


def gram_kernel(x, out, acc):
    step = pl.program_id(0)

    @pl.when(step == 0)
    def _():
        acc[...] = jnp.zeros_like(acc)

    tile = x[...]
    acc[...] += tn(tile, tile)

    @pl.when(step == pl.num_programs(0) - 1)
    def _():
        out[...] = acc[...].astype(out.dtype)


def gram(x):
    tokens = x.shape[0]
    chunk = 512
    return pl.pallas_call(
        gram_kernel,
        grid=(tokens // chunk,),
        out_shape=jax.ShapeDtypeStruct((block, block), jnp.bfloat16),
        in_specs=[pl.BlockSpec((chunk, block), lambda i: (i, 0))],
        out_specs=pl.BlockSpec((block, block), lambda i: (0, 0)),
        scratch_shapes=[pltpu.VMEM((block, block), jnp.float32)],
        compiler_params=pltpu.CompilerParams(vmem_limit_bytes=40 * mib),
        cost_estimate=cost(2 * tokens * block * block, 2 * tokens * block + 2 * block * block),
    )(x)


def rotate_kernel(own, w, right, out):
    half = block // 2
    for p in range(w.shape[1]):
        left = jnp.concatenate([w[own[0] ^ j, p] for j in range(4)], axis=0)
        upper = right[:4, p].reshape(-1, half)
        lower = right[4:, p].reshape(-1, half)
        y = nt(upper, left[:, :half]) + nt(lower, left[:, half:])
        out[:, p] = y.astype(out.dtype).reshape(out.shape[0], rows, -1)


def rotate(own, w, right):
    pairs = w.shape[1]
    return pl.pallas_call(
        rotate_kernel,
        out_shape=jax.ShapeDtypeStruct((8, pairs, rows, 4 * rows), jnp.bfloat16),
        in_specs=[pl.BlockSpec(memory_space=pltpu.SMEM)] + in_vmem(2),
        out_specs=in_vmem(1)[0],
        compiler_params=pltpu.CompilerParams(vmem_limit_bytes=24 * mib),
        cost_estimate=cost(2 * pairs * 256 * 128 * block, 5 * mib // 2),
    )(own, w, right)


def middle_kernel(x, left_t, vals_left, vals_right, out):
    groups, pairs = x.shape[0], x.shape[1]
    width = x.shape[3]
    slab = jnp.concatenate([x[i].reshape(pairs * rows, width) for i in range(groups)], axis=1)
    inner = nt(slab, left_t[...]).astype(jnp.bfloat16)
    denom = vals_right[...] * vals_left[...] + damping
    scaled = (inner.astype(jnp.float32) / denom).astype(jnp.bfloat16)
    back = jnp.dot(scaled, left_t[...], preferred_element_type=jnp.float32).astype(out.dtype)
    for i in range(groups):
        out[i] = back[:, i * width : (i + 1) * width].reshape(pairs, rows, width)


def middle(x, left_t, vals_left, vals_right):
    return pl.pallas_call(
        middle_kernel,
        out_shape=jax.ShapeDtypeStruct(x.shape, x.dtype),
        in_specs=in_vmem(4),
        out_specs=in_vmem(1)[0],
        compiler_params=pltpu.CompilerParams(vmem_limit_bytes=24 * mib),
        cost_estimate=cost(4 * 96 * block * block, 5 * mib // 2),
    )(x, left_t, vals_left, vals_right)


def restore_kernel(x, right, out):
    half = block // 2
    for p in range(x.shape[1]):
        back_t = x[:, p].reshape(-1, x.shape[3])
        upper = right[:4, p].reshape(-1, half)
        lower = right[4:, p].reshape(-1, half)
        out[:, p, :, :half] = tn(back_t, upper).astype(out.dtype).reshape(4, rows, half)
        out[:, p, :, half:] = tn(back_t, lower).astype(out.dtype).reshape(4, rows, half)


def restore(x, right):
    pairs = x.shape[1]
    return pl.pallas_call(
        restore_kernel,
        out_shape=jax.ShapeDtypeStruct((4, pairs, rows, block), x.dtype),
        in_specs=in_vmem(2),
        out_specs=in_vmem(1)[0],
        compiler_params=pltpu.CompilerParams(vmem_limit_bytes=24 * mib),
        cost_estimate=cost(2 * pairs * 256 * 128 * block, 5 * mib // 2),
    )(x, right)


def total(x):
    return jnp.sum(x.astype(jnp.float32), axis=0)


def spread(x, names, count):
    copies = jnp.broadcast_to(x[None], (count,) + x.shape)
    return lax.all_to_all(copies, names, split_axis=0, concat_axis=0, tiled=True)


def body(
    layer_inputs,
    output_grads,
    slot_block_table,
    weight_gradient_pairs,
    basis_in,
    basis_out,
    values_in,
    values_out,
):
    tokens_dev = layer_inputs.shape[0]
    count_out = values_out.shape[0]
    pairs = weight_gradient_pairs.shape[0]
    cols = basis_out.shape[2]
    total_tokens = tokens_dev * n_dp * n_fsdp

    there = [
        (z * 32 + h * 16 + f, f * 32 + h * 16 + z)
        for z in range(16)
        for h in range(2)
        for f in range(16)
    ]
    back_again = [(b, a) for a, b in there]

    position = lax.axis_index(fsdp) * pairs
    left_cols = lax.dynamic_index_in_dim(basis_in, position // count_out, 0, keepdims=False)
    left_rows = jnp.transpose(left_cols.reshape(4, 4, 2, rows, rows), (4, 2, 1, 0, 3))

    w = weight_gradient_pairs.reshape(pairs, rows, 16, 2, rows)
    w = jnp.transpose(w, (0, 1, 3, 2, 4)).reshape(pairs, rows, block)
    moved = lax.ppermute(
        jnp.concatenate([w, left_rows.reshape(1, rows, block)], axis=0), axes, there
    )

    groups = count_out // pairs
    here = lax.axis_index("z")
    wanted = basis_out.reshape(groups, pairs * rows * cols // 128, 128)
    pieces = []
    for m in range(4):
        piece = lax.dynamic_index_in_dim(wanted, (here ^ m) % groups, 0, keepdims=False)
        pieces.append(lax.ppermute(piece, "z", [(i, i ^ m) for i in range(16)]) if m else piece)
    pieces = jnp.stack(pieces)
    far = [lax.ppermute(pieces, "z", [(i, i ^ m) for i in range(16)]) for m in (4, 8, 12)]
    came = jnp.concatenate([pieces] + far)
    moved, came = lax.optimization_barrier((moved, came))
    w = moved[:pairs]
    left_t = lax.all_gather(moved[pairs], plane, axis=0, tiled=True)
    others = [
        lax.ppermute(w, col_group, [(j, j ^ m) for j in range(4)]) for m in range(1, 4)
    ]
    w = jnp.stack([w] + others)
    came = jnp.take(came, here ^ jnp.arange(16), axis=0, mode="clip")
    came = jnp.transpose(came.reshape(16, pairs, rows, cols), (1, 3, 0, 2))
    came = came.reshape(pairs, cols, block // 2)

    sorted_slots = sort_slots(slot_block_table, layer_inputs, output_grads)
    gathered = lax.all_to_all(sorted_slots, fsdp, split_axis=0, concat_axis=0, tiled=True)
    gathered, w, came = lax.optimization_barrier((gathered, w, came))
    right = spread(came, row_group, 8)
    partial = gram(gathered.reshape(-1, block))
    mine = lax.psum_scatter(partial, "z", scatter_dimension=0, tiled=True)
    mine = mine.reshape(2, rows, block)
    own = lax.axis_index("xh")
    sent = lax.dynamic_index_in_dim(mine, 1 - own, 0, keepdims=True)
    kept = lax.dynamic_index_in_dim(mine, own, 0, keepdims=True)
    came_cov = lax.ppermute(sent, "xh", [(0, 1), (1, 0)])
    covariance = (kept.astype(jnp.float32) + came_cov.astype(jnp.float32)) / total_tokens

    pair = lax.axis_index("z") * pairs
    start = lax.axis_index(col_group) * 256 + lax.axis_index(row_group) * rows
    right_vals = lax.dynamic_slice(values_out, (pair % count_out, start), (pairs, rows))
    left_vals = lax.dynamic_index_in_dim(values_in, pair // count_out, 0, keepdims=False)
    left_vals = jnp.transpose(left_vals.reshape(16, 2, rows), (1, 0, 2))

    rotated = rotate(lax.axis_index(col_group).reshape(1), w, right)
    slab = lax.all_to_all(rotated, row_group, split_axis=0, concat_axis=0, tiled=True)
    back_rot = middle(
        slab, left_t, left_vals.reshape(1, block), right_vals.reshape(pairs * rows, 1)
    )
    again = lax.all_to_all(back_rot, row_group, split_axis=0, concat_axis=0, tiled=True)
    parts = restore(again, right)
    parts = lax.all_to_all(parts, col_group, split_axis=0, concat_axis=0, tiled=True)
    result = total(parts).astype(jnp.bfloat16).reshape(pairs, rows, 2, 16, rows)
    result = jnp.transpose(result, (0, 1, 3, 2, 4)).reshape(pairs, rows, block)
    preconditioned = lax.ppermute(result, axes, back_again)
    return covariance, preconditioned


def solution(mesh):
    fine = Mesh(mesh.devices.reshape(sizes), axes)
    everywhere = P(axes, None)
    placed = (
        everywhere,
        everywhere,
        P(),
        P(fsdp, dp, None),
        P(None, None, dp),
        P(None, dp, fsdp),
        P(),
        P(),
    )
    return jax.shard_map(
        body,
        mesh=fine,
        in_specs=placed,
        out_specs=(P(fsdp, dp, None), P(fsdp, dp, None)),
        check_vma=False,
    )
```

time: 1020 us -> 239 us (0.23)
  waiting for transfers between devices: 903 us -> 97.9 us
  starting transfers between devices: 22.6 us -> 66.8 us
  matrix products: 30.2 us -> 0 us
  blocking collectives: 13.3 us -> 25.1 us
  local copies, waits for them, and re-layouts: 30.3 us -> 19.3 us
  Pallas kernels: 0 us -> 10.9 us
    reduce_scatter x1, waiting for transfers between devices: 633 us -> 0.03 us  [body(): mine = lax.psum_scatter(partial, 'z', scatter_dimension=0, tiled=True)]
    all_gather x2 -> x1, waiting for transfers between devices: 195 us -> 0.02 us  [body(): left_t = lax.all_gather(moved[pairs], plane, axis=0, tiled=True)]
    ppermute x0 -> x12, waiting for transfers between devices: none -> 69.4 us  [the longest x3 34.6 us: body(): lax.ppermute(pieces, 'z', [(i, i ^ m) for i in range(16)])]
    ppermute x0 -> x12, starting transfers between devices: none -> 48.3 us  [the longest x3 17.7 us: body(): lax.ppermute(pieces, 'z', [(i, i ^ m) for i in range(16)])]
    all_to_all x3, waiting for transfers between devices: 73.8 us -> 28.5 us  [the longest x1 24 us: spread(): lax.all_to_all(copies, names, split_axis=0, concat_axis=0, tiled=True)]
    dot_general x6 -> x0, matrix products: 30.2 us -> none  [the longest x1 13.2 us: body(): jnp.einsum('tsb,tsc->sbc', gathered_tokens, gathered_tokens, preferred_el...]
    all_to_all x1 -> x2, blocking collectives: 13.3 us -> 25.1 us  [the longest x1 15.6 us: body(): lax.all_to_all(parts, col_group, split_axis=0, concat_axis=0, tiled=True)]
    pallas_call x0 -> x5, Pallas kernels: none -> 10.9 us  [the longest x1 6.94 us: gram(): pl.pallas_call(gram_kernel, grid=(tokens // chunk,), out_shape=jax.ShapeD...]
  transfers between devices with their start and end apart: 6 -> 17, of which waited for: 5 -> 7; matrix products, arithmetic and copies ran while one was open for 5% -> 4% of each run, Pallas kernels for 0% -> 4%
where the time goes in v1:
time: 239 us; the launch traced here: 238 us
  waiting for transfers between devices  97.9 us (41%)
  starting transfers between devices  66.8 us (28%)
  blocking collectives  25.1 us (11%)
  local copies, waits for them, and re-layouts  19.3 us (8%)
  between operations  16.1 us (7%)
  Pallas kernels  10.9 us (5%)
    ppermute x3, waiting for transfers between devices, body(): lax.ppermute(pieces, 'z', [(i, i ^ m) for i in range(16)])  34.6 us
    ppermute x1, waiting for transfers between devices, body(): preconditioned = lax.ppermute(result, axes, back_again)  27.8 us
    all_to_all x1, waiting for transfers between devices, spread(): lax.all_to_all(copies, names, split_axis=0, concat_axis=0, tiled=True)  24 us
    ppermute x3, starting transfers between devices, body(): lax.ppermute(pieces, 'z', [(i, i ^ m) for i in range(16)])  17.7 us
    all_to_all x1, blocking collectives, body(): lax.all_to_all(parts, col_group, split_axis=0, concat_axis=0, tiled=True)  15.6 us
    ppermute x3, starting transfers between devices, body(): lax.ppermute(w, col_group, [(j, j ^ m) for j in range(4)])  10.7 us
    all_to_all x1, starting transfers between devices, body(): lax.all_to_all(sorted_slots, fsdp, split_axis=0, concat_axis=0, tiled=True)  10.2 us
    ppermute x3, starting transfers between devices, body(): lax.ppermute(piece, 'z', [(i, i ^ m) for i in range(16)])  10.1 us
  transfers between devices with their start and end apart: 17, of which 7 were waited for; matrix products, arithmetic and copies ran while one was open for 4% of the time, Pallas kernels for 4%

profile of v1, /device:TPU:8, one launch (start us, length us, event | category | flops | bytes accessed | tf_op | source)
XLA Modules:
  0.0 237.9 jit_solution(9479017308276939858)
XLA Ops:
  8.0 1.9 copy-done.2
  9.9 1.2 copy-done.5
  11.2 0.7 copy-done.6
  11.8 1.2 shard_map.95
  13.0 2.0 copy-done.1
  15.1 10.2 %all-to-all-start = ((bf16[16,128,1024]{2,1,0:T(8,128)(2,1)}), bf16[16,128,1024]{2,1,0:T(8,128)(2,1)}, u32[]{:S(2)}, u32[]{:S(2)}) async-start(bf16[16,128,1024]{2,1,0:T(8,128)(2,1)} %copy-done.1), calls=%async_computation | async-start | bytes 8388608 | tf_op jit(solution)/shard_map/all_to_all | solution.py:244
  25.6 1.9 collective-permute-start.1
  27.5 2.8 %collective-permute-start.2 = (bf16[48,128]{1,0:T(8,128)(2,1)S(1)}, bf16[48,128]{1,0:T(8,128)(2,1)S(1)}, u32[]{:S(2)}, u32[]{:S(2)}) collective-permute-start(bf16[48,128]{1,0:T(8,128)(2,1)S(1)} %get-tuple-element.17), channel_id=1, source_target_pairs={{0,64},{32,96},{64,0},{96,32},{128,192},{160,224},{192,128},{224,1... | collective-permute-start | bytes 36872 | tf_op jit(solution)/shard_map/ppermute | solution.py:228
  30.4 5.3 %collective-permute-start.3 = (bf16[48,128]{1,0:T(8,128)(2,1)S(1)}, bf16[48,128]{1,0:T(8,128)(2,1)S(1)}, u32[]{:S(2)}, u32[]{:S(2)}) collective-permute-start(bf16[48,128]{1,0:T(8,128)(2,1)S(1)} %get-tuple-element.16), channel_id=1, source_target_pairs={{0,96},{32,64},{64,32},{96,0},{128,224},{160,192},{192,160},{224,1... | collective-permute-start | bytes 36872 | tf_op jit(solution)/shard_map/ppermute | solution.py:228
  36.4 0.6 reshape.59
  37.1 0.8 reshape.60
  37.9 1.9 collective-permute-start
  39.9 6.9 %collective-permute-start.4 = (bf16[4,48,128]{2,1,0:T(8,128)(2,1)S(1)}, bf16[4,48,128]{2,1,0:T(8,128)(2,1)S(1)}, u32[]{:S(2)}, u32[]{:S(2)}) collective-permute-start(bf16[4,48,128]{2,1,0:T(8,128)(2,1)S(1)} %pad_maximum_fusion.2), channel_id=1, source_target_pairs={{0,128},{32,160},{64,192},{96,224},{128,0},{160,32},{192,64},{224,... | collective-permute-start | bytes 147464 | tf_op jit(solution)/shard_map/ppermute | solution.py:230
  46.9 8.8 %collective-permute-start.5 = (bf16[4,48,128]{2,1,0:T(8,128)(2,1)S(1)}, bf16[4,48,128]{2,1,0:T(8,128)(2,1)S(1)}, u32[]{:S(2)}, u32[]{:S(2)}) collective-permute-start(bf16[4,48,128]{2,1,0:T(8,128)(2,1)S(1)} %pad_maximum_fusion.2), channel_id=1, source_target_pairs={{0,256},{32,288},{64,320},{96,352},{128,384},{160,416},{192,448},{... | collective-permute-start | bytes 147464 | tf_op jit(solution)/shard_map/ppermute | solution.py:230
  55.7 1.9 collective-permute-start.6
  57.7 34.6 %collective-permute-done.4 = bf16[4,48,128]{2,1,0:T(8,128)(2,1)S(1)} collective-permute-done((bf16[4,48,128]{2,1,0:T(8,128)(2,1)S(1)}, bf16[4,48,128]{2,1,0:T(8,128)(2,1)S(1)}, u32[]{:S(2)}, u32[]{:S(2)}) %collective-permute-start.4) | collective-permute-done | bytes 49184 | tf_op jit(solution)/shard_map/ppermute | solution.py:230
  92.4 0.6 slice.7
  93.1 5.4 %collective-permute-start.9 = (bf16[3,32,1024]{2,1,0:T(8,128)(2,1)S(1)}, bf16[3,32,1024]{2,1,0:T(8,128)(2,1)S(1)}, u32[]{:S(2)}, u32[]{:S(2)}) collective-permute-start(bf16[3,32,1024]{2,1,0:T(8,128)(2,1)S(1)} %get-tuple-element.15), channel_id=1, source_target_pairs={{0,12},{4,8},{8,4},{12,0},{1,13},{5,9},{9,5},{13,1},{2,14},{6,10},... | collective-permute-start | bytes 589832 | tf_op jit(solution)/shard_map/ppermute | solution.py:236
  98.6 1.9 collective-permute-start.8
  100.5 3.4 %collective-permute-start.7 = (bf16[3,32,1024]{2,1,0:T(8,128)(2,1)S(1)}, bf16[3,32,1024]{2,1,0:T(8,128)(2,1)S(1)}, u32[]{:S(2)}, u32[]{:S(2)}) collective-permute-start(bf16[3,32,1024]{2,1,0:T(8,128)(2,1)S(1)} %get-tuple-element.15), channel_id=1, source_target_pairs={{0,4},{4,0},{8,12},{12,8},{1,5},{5,1},{9,13},{13,9},{2,6},{6,2},{1... | collective-permute-start | bytes 589832 | tf_op jit(solution)/shard_map/ppermute | solution.py:236
  103.9 0.6 gather_fusion
  104.7 0.4 collective-permute-done.9
  105.1 3.0 %collective-permute-done.8 = bf16[3,32,1024]{2,1,0:T(8,128)(2,1)S(1)} collective-permute-done((bf16[3,32,1024]{2,1,0:T(8,128)(2,1)S(1)}, bf16[3,32,1024]{2,1,0:T(8,128)(2,1)S(1)}, u32[]{:S(2)}, u32[]{:S(2)}) %collective-permute-start.8) | collective-permute-done | bytes 196640 | tf_op jit(solution)/shard_map/ppermute | solution.py:236
  108.1 3.4 %collective-permute-done.7 = bf16[3,32,1024]{2,1,0:T(8,128)(2,1)S(1)} collective-permute-done((bf16[3,32,1024]{2,1,0:T(8,128)(2,1)S(1)}, bf16[3,32,1024]{2,1,0:T(8,128)(2,1)S(1)}, u32[]{:S(2)}, u32[]{:S(2)}) %collective-permute-start.7) | collective-permute-done | bytes 196640 | tf_op jit(solution)/shard_map/ppermute | solution.py:236
  111.7 6.9 %shard_map.96 = bf16[1024,1024]{1,0:T(8,128)(2,1)S(1)} custom-call(bf16[2048,1024]{1,0:T(8,128)(2,1)} %bitcast.15.x), custom_call_target="tpu_custom_call" | custom-call | flops 4294967296 | bytes 6291456 | tf_op jit(solution)/shard_map/pallas_call | solution.py:100
  118.6 1.3 copy-done.4
  120.2 1.3 broadcast_in_dim.4
  121.5 4.3 %all-to-all-start.1 = ((bf16[8,3,64,512]{3,2,1,0:T(8,128)(2,1)}), bf16[8,3,64,512]{3,2,1,0:T(8,128)(2,1)S(1)}, u32[]{:S(2)}, u32[]{:S(2)}) async-start(bf16[8,3,64,512]{3,2,1,0:T(8,128)(2,1)} %broadcast_in_dim.4), calls=%async_computation.2 | async-start | bytes 3145728 | tf_op jit(solution)/shard_map/all_to_all | solution.py:185
  125.8 24.0 %all-to-all-done.1.right = bf16[8,3,64,512]{3,2,1,0:T(8,128)(2,1)S(1)} async-done(((bf16[8,3,64,512]{3,2,1,0:T(8,128)(2,1)}), bf16[8,3,64,512]{3,2,1,0:T(8,128)(2,1)S(1)}, u32[]{:S(2)}, u32[]{:S(2)}) %all-to-all-start.1) | async-done | bytes 1572896 | tf_op jit(solution)/shard_map/all_to_all | solution.py:185
  149.8 1.2 shard_map.97
  151.1 3.8 %all-to-all-start.2 = ((bf16[8,3,32,128]{3,2,1,0:T(8,128)(2,1)}), bf16[8,3,32,128]{3,2,1,0:T(8,128)(2,1)S(1)}, u32[]{:S(2)}, u32[]{:S(2)}) async-start(bf16[8,3,32,128]{3,2,1,0:T(8,128)(2,1)} %shard_map.97), calls=%async_computation.3 | async-start | bytes 393216 | tf_op jit(solution)/shard_map/all_to_all | solution.py:263
  154.9 0.7 dynamic-slice_reduce_fusion
  155.8 0.8 dynamic_slice.39
  156.7 4.5 %all-to-all-done.2.x = bf16[8,3,32,128]{3,2,1,0:T(8,128)(2,1)S(1)} async-done(((bf16[8,3,32,128]{3,2,1,0:T(8,128)(2,1)}), bf16[8,3,32,128]{3,2,1,0:T(8,128)(2,1)S(1)}, u32[]{:S(2)}, u32[]{:S(2)}) %all-to-all-start.2) | async-done | bytes 196640 | tf_op jit(solution)/shard_map/all_to_all | solution.py:263
  161.2 1.6 copy-done.3
  162.8 1.1 shard_map.98
  163.9 9.6 %all_to_all.25.x = bf16[8,3,32,128]{3,2,1,0:T(8,128)(2,1)S(1)} all-to-all(bf16[8,3,32,128]{3,2,1,0:T(8,128)(2,1)S(1)} %shard_map.98), channel_id=1, replica_groups=mesh['z'=16,'xh'=2,'xl'=2,'yh'=2,'yl'=2,'c'=2] {'xh','yl','c'}, dimensions={0} | all-to-all | bytes 393216 | tf_op jit(solution)/shard_map/all_to_all | solution.py:267
  173.5 0.4 shard_map.99
  173.9 15.6 %all_to_all.26 = bf16[4,3,32,1024]{3,2,1,0:T(8,128)(2,1)S(1)} all-to-all(bf16[4,3,32,1024]{3,2,1,0:T(8,128)(2,1)S(1)} %shard_map.99), channel_id=1, replica_groups=mesh['z'=16,'xh'=2,'xl'=2,'yh'=2,'yl'=2,'c'=2] {'xl','yh'}, dimensions={0} | all-to-all | bytes 1572864 | tf_op jit(solution)/shard_map/all_to_all | solution.py:269
  189.6 0.6 reshape.72
  190.1 0.7 copy.24
  190.8 0.8 reshape.73
  191.6 4.0 %collective-permute-start.11 = (bf16[3,32,1024]{2,1,0:T(8,128)(2,1)S(1)}, bf16[3,32,1024]{2,1,0:T(8,128)(2,1)S(1)}, u32[]{:S(2)}, u32[]{:S(2)}) collective-permute-start(bf16[3,32,1024]{2,1,0:T(8,128)(2,1)S(1)} %reshape.73), channel_id=1, source_target_pairs={{0,0},{32,1},{64,2},{96,3},{128,4},{160,5},{192,6},{224,7},{256,8}... | collective-permute-start | bytes 589832 | tf_op jit(solution)/shard_map/ppermute | solution.py:272
  195.7 0.8 constant_dynamic-slice_fusion
  196.5 3.9 %collective-permute-start.10 = (bf16[1,32,1024]{2,1,0:T(8,128)(2,1)S(1)}, bf16[1,32,1024]{2,1,0:T(8,128)(2,1)S(1)}, u32[]{:S(2)}, u32[]{:S(2)}) collective-permute-start(bf16[1,32,1024]{2,1,0:T(8,128)(2,1)S(1)} %constant_dynamic-slice_fusion), channel_id=1, source_target_pairs={{0,16},{16,0},{1,17},{17,1},{2,18},{18,2},{3,19},{19,3},{4,20},{20... | collective-permute-start | bytes 196616 | tf_op jit(solution)/shard_map/ppermute | solution.py:253
  200.4 27.8 %collective-permute-done.11 = bf16[3,32,1024]{2,1,0:T(8,128)(2,1)S(1)} collective-permute-done((bf16[3,32,1024]{2,1,0:T(8,128)(2,1)S(1)}, bf16[3,32,1024]{2,1,0:T(8,128)(2,1)S(1)}, u32[]{:S(2)}, u32[]{:S(2)}) %collective-permute-start.11) | collective-permute-done | bytes 196640 | tf_op jit(solution)/shard_map/ppermute | solution.py:272
  228.2 1.5 add_multiply_fusion
  229.8 0.7 copy.34
  (53 shorter events, 2.1 us)
Async XLA Ops:
  8.0 27.8 %copy-start = (bf16[4,1024,32]{1,2,0:T(8,128)(2,1)S(1)}, bf16[4,1024,32]{1,2,0:T(8,128)(2,1)}, u32[]{:S(2)}) copy-start(bf16[4,1024,32]{1,2,0:T(8,128)(2,1)} %param.12) | copy-start | bytes 786436
  8.0 1.9 copy-start.2
  9.9 1.2 copy-start.5
  11.2 0.7 copy-start.6
  13.0 2.0 copy-start.1
  15.1 10.4 %copy-start.8 = (bf16[12,32,64]{2,1,0:T(8,128)(2,1)S(1)}, bf16[12,32,64]{2,1,0:T(8,128)(2,1)}, u32[]{:S(2)}) copy-start(bf16[12,32,64]{2,1,0:T(8,128)(2,1)} %param.13) | copy-start | bytes 147460
  15.1 21.3 %copy-start.7 = (bf16[3,32,1024]{2,1,0:T(8,128)(2,1)S(1)}, bf16[3,32,1024]{2,1,0:T(8,128)(2,1)}, u32[]{:S(2)}) copy-start(bf16[3,32,1024]{2,1,0:T(8,128)(2,1)} %param.11) | copy-start | bytes 589828
  15.1 96.6 %all-to-all-start = ((bf16[16,128,1024]{2,1,0:T(8,128)(2,1)}), bf16[16,128,1024]{2,1,0:T(8,128)(2,1)}, u32[]{:S(2)}, u32[]{:S(2)}) async-start(bf16[16,128,1024]{2,1,0:T(8,128)(2,1)} %copy-done.1), calls=%async_computation | async-start | bytes 8388608 | tf_op jit(solution)/shard_map/all_to_all | solution.py:244
  25.3 131.4 %all-gather.3.cloned.1.call-start = ((), (), s32[]{:S(2)}) async-start(), calls=%async_computation.7 | async-start | bytes 2162688 | tf_op jit(solution)/shard_map/all_gather | solution.py:234
  25.6 14.3 %collective-permute-start.1 = (bf16[48,128]{1,0:T(8,128)(2,1)S(1)}, bf16[48,128]{1,0:T(8,128)(2,1)S(1)}, u32[]{:S(2)}, u32[]{:S(2)}) collective-permute-start(bf16[48,128]{1,0:T(8,128)(2,1)S(1)} %get-tuple-element.18), channel_id=1, source_target_pairs={{0,32},{32,0},{64,96},{96,64},{128,160},{160,128},{192,224},{224,1... | collective-permute-start | bytes 36872 | tf_op jit(solution)/shard_map/ppermute | solution.py:228
  27.5 12.4 %collective-permute-start.2 = (bf16[48,128]{1,0:T(8,128)(2,1)S(1)}, bf16[48,128]{1,0:T(8,128)(2,1)S(1)}, u32[]{:S(2)}, u32[]{:S(2)}) collective-permute-start(bf16[48,128]{1,0:T(8,128)(2,1)S(1)} %get-tuple-element.17), channel_id=1, source_target_pairs={{0,64},{32,96},{64,0},{96,32},{128,192},{160,224},{192,128},{224,1... | collective-permute-start | bytes 36872 | tf_op jit(solution)/shard_map/ppermute | solution.py:228
  30.4 9.5 %collective-permute-start.3 = (bf16[48,128]{1,0:T(8,128)(2,1)S(1)}, bf16[48,128]{1,0:T(8,128)(2,1)S(1)}, u32[]{:S(2)}, u32[]{:S(2)}) collective-permute-start(bf16[48,128]{1,0:T(8,128)(2,1)S(1)} %get-tuple-element.16), channel_id=1, source_target_pairs={{0,96},{32,64},{64,32},{96,0},{128,224},{160,192},{192,160},{224,1... | collective-permute-start | bytes 36872 | tf_op jit(solution)/shard_map/ppermute | solution.py:228
  37.9 54.4 %collective-permute-start = (bf16[4,32,1024]{2,1,0:T(8,128)(2,1)S(1)}, bf16[4,32,1024]{2,1,0:T(8,128)(2,1)S(1)}, u32[]{:S(2)}, u32[]{:S(2)}) collective-permute-start(bf16[4,32,1024]{2,1,0:T(8,128)(2,1)S(1)} %pad_maximum_fusion.1), channel_id=1, source_target_pairs={{0,0},{1,32},{2,64},{3,96},{4,128},{5,160},{6,192},{7,224},{8,256}... | collective-permute-start | bytes 786440 | tf_op jit(solution)/shard_map/ppermute | solution.py:218
  39.9 52.4 %collective-permute-start.4 = (bf16[4,48,128]{2,1,0:T(8,128)(2,1)S(1)}, bf16[4,48,128]{2,1,0:T(8,128)(2,1)S(1)}, u32[]{:S(2)}, u32[]{:S(2)}) collective-permute-start(bf16[4,48,128]{2,1,0:T(8,128)(2,1)S(1)} %pad_maximum_fusion.2), channel_id=1, source_target_pairs={{0,128},{32,160},{64,192},{96,224},{128,0},{160,32},{192,64},{224,... | collective-permute-start | bytes 147464 | tf_op jit(solution)/shard_map/ppermute | solution.py:230
  46.9 45.5 %collective-permute-start.5 = (bf16[4,48,128]{2,1,0:T(8,128)(2,1)S(1)}, bf16[4,48,128]{2,1,0:T(8,128)(2,1)S(1)}, u32[]{:S(2)}, u32[]{:S(2)}) collective-permute-start(bf16[4,48,128]{2,1,0:T(8,128)(2,1)S(1)} %pad_maximum_fusion.2), channel_id=1, source_target_pairs={{0,256},{32,288},{64,320},{96,352},{128,384},{160,416},{192,448},{... | collective-permute-start | bytes 147464 | tf_op jit(solution)/shard_map/ppermute | solution.py:230
  55.7 36.7 %collective-permute-start.6 = (bf16[4,48,128]{2,1,0:T(8,128)(2,1)S(1)}, bf16[4,48,128]{2,1,0:T(8,128)(2,1)S(1)}, u32[]{:S(2)}, u32[]{:S(2)}) collective-permute-start(bf16[4,48,128]{2,1,0:T(8,128)(2,1)S(1)} %pad_maximum_fusion.2), channel_id=1, source_target_pairs={{0,384},{32,416},{64,448},{96,480},{128,256},{160,288},{192,320},{... | collective-permute-start | bytes 147464 | tf_op jit(solution)/shard_map/ppermute | solution.py:230
  93.0 102.6 %reduce-scatter.2.cloned.1.call-start = ((), (), s32[]{:S(2)}) async-start(), calls=%async_computation.6 | async-start | bytes 2228224 | tf_op jit(solution)/shard_map/reduce_scatter | solution.py:248
  93.1 12.0 %collective-permute-start.9 = (bf16[3,32,1024]{2,1,0:T(8,128)(2,1)S(1)}, bf16[3,32,1024]{2,1,0:T(8,128)(2,1)S(1)}, u32[]{:S(2)}, u32[]{:S(2)}) collective-permute-start(bf16[3,32,1024]{2,1,0:T(8,128)(2,1)S(1)} %get-tuple-element.15), channel_id=1, source_target_pairs={{0,12},{4,8},{8,4},{12,0},{1,13},{5,9},{9,5},{13,1},{2,14},{6,10},... | collective-permute-start | bytes 589832 | tf_op jit(solution)/shard_map/ppermute | solution.py:236
  98.6 9.6 %collective-permute-start.8 = (bf16[3,32,1024]{2,1,0:T(8,128)(2,1)S(1)}, bf16[3,32,1024]{2,1,0:T(8,128)(2,1)S(1)}, u32[]{:S(2)}, u32[]{:S(2)}) collective-permute-start(bf16[3,32,1024]{2,1,0:T(8,128)(2,1)S(1)} %get-tuple-element.15), channel_id=1, source_target_pairs={{0,8},{4,12},{8,0},{12,4},{1,9},{5,13},{9,1},{13,5},{2,10},{6,14},... | collective-permute-start | bytes 589832 | tf_op jit(solution)/shard_map/ppermute | solution.py:236
  100.5 11.1 %collective-permute-start.7 = (bf16[3,32,1024]{2,1,0:T(8,128)(2,1)S(1)}, bf16[3,32,1024]{2,1,0:T(8,128)(2,1)S(1)}, u32[]{:S(2)}, u32[]{:S(2)}) collective-permute-start(bf16[3,32,1024]{2,1,0:T(8,128)(2,1)S(1)} %get-tuple-element.15), channel_id=1, source_target_pairs={{0,4},{4,0},{8,12},{12,8},{1,5},{5,1},{9,13},{13,9},{2,6},{6,2},{1... | collective-permute-start | bytes 589832 | tf_op jit(solution)/shard_map/ppermute | solution.py:236
  118.6 1.3 copy-start.4
  121.5 28.4 %all-to-all-start.1 = ((bf16[8,3,64,512]{3,2,1,0:T(8,128)(2,1)}), bf16[8,3,64,512]{3,2,1,0:T(8,128)(2,1)S(1)}, u32[]{:S(2)}, u32[]{:S(2)}) async-start(bf16[8,3,64,512]{3,2,1,0:T(8,128)(2,1)} %broadcast_in_dim.4), calls=%async_computation.2 | async-start | bytes 3145728 | tf_op jit(solution)/shard_map/all_to_all | solution.py:185
  151.1 10.1 %all-to-all-start.2 = ((bf16[8,3,32,128]{3,2,1,0:T(8,128)(2,1)}), bf16[8,3,32,128]{3,2,1,0:T(8,128)(2,1)S(1)}, u32[]{:S(2)}, u32[]{:S(2)}) async-start(bf16[8,3,32,128]{3,2,1,0:T(8,128)(2,1)} %shard_map.97), calls=%async_computation.3 | async-start | bytes 393216 | tf_op jit(solution)/shard_map/all_to_all | solution.py:263
  161.2 1.6 copy-start.3
  191.6 36.6 %collective-permute-start.11 = (bf16[3,32,1024]{2,1,0:T(8,128)(2,1)S(1)}, bf16[3,32,1024]{2,1,0:T(8,128)(2,1)S(1)}, u32[]{:S(2)}, u32[]{:S(2)}) collective-permute-start(bf16[3,32,1024]{2,1,0:T(8,128)(2,1)S(1)} %reshape.73), channel_id=1, source_target_pairs={{0,0},{32,1},{64,2},{96,3},{128,4},{160,5},{192,6},{224,7},{256,8}... | collective-permute-start | bytes 589832 | tf_op jit(solution)/shard_map/ppermute | solution.py:272
  196.5 31.7 %collective-permute-start.10 = (bf16[1,32,1024]{2,1,0:T(8,128)(2,1)S(1)}, bf16[1,32,1024]{2,1,0:T(8,128)(2,1)S(1)}, u32[]{:S(2)}, u32[]{:S(2)}) collective-permute-start(bf16[1,32,1024]{2,1,0:T(8,128)(2,1)S(1)} %constant_dynamic-slice_fusion), channel_id=1, source_target_pairs={{0,16},{16,0},{1,17},{17,1},{2,18},{18,2},{3,19},{19,3},{4,20},{20... | collective-permute-start | bytes 196616 | tf_op jit(solution)/shard_map/ppermute | solution.py:253
Sparse Core Ops, SparseCore 0:
  93.2 60.1 all-gather.2
Sparse Core Ops, SparseCore 1:
  120.1 72.2 reduce-scatter.1

commit v2 on v1

--- a/solution.py
+++ b/solution.py
@@ -202,15 +202,19 @@
     total_tokens = tokens_dev * n_dp * n_fsdp
 
     there = [
-        (z * 32 + h * 16 + f, f * 32 + h * 16 + z)
+        (z * 32 + h * 16 + f, f * 32 + h * 16 + (z ^ f))
         for z in range(16)
         for h in range(2)
         for f in range(16)
     ]
     back_again = [(b, a) for a, b in there]
 
-    position = lax.axis_index(fsdp) * pairs
-    left_cols = lax.dynamic_index_in_dim(basis_in, position // count_out, 0, keepdims=False)
+    order = jnp.arange(16)
+    target = lax.axis_index(fsdp)
+    left_cols = lax.dynamic_index_in_dim(
+        basis_in, target * pairs // count_out, 0, keepdims=False
+    )
+    left_cols = jnp.take(left_cols.reshape(16, 2 * rows, rows), target ^ order, axis=0, mode="clip")
     left_rows = jnp.transpose(left_cols.reshape(4, 4, 2, rows, rows), (4, 2, 1, 0, 3))
 
     w = weight_gradient_pairs.reshape(pairs, rows, 16, 2, rows)
@@ -232,18 +236,18 @@
     moved, came = lax.optimization_barrier((moved, came))
     w = moved[:pairs]
     left_t = lax.all_gather(moved[pairs], plane, axis=0, tiled=True)
+    came = jnp.take(came, here ^ order, axis=0, mode="clip")
+    came = jnp.transpose(came.reshape(16, pairs, rows, cols), (1, 3, 0, 2))
+    came = came.reshape(pairs, cols, block // 2)
+
+    sorted_slots = sort_slots(slot_block_table, layer_inputs, output_grads)
+    gathered = lax.all_to_all(sorted_slots, fsdp, split_axis=0, concat_axis=0, tiled=True)
+    gathered, w, came = lax.optimization_barrier((gathered, w, came))
+    right = spread(came, row_group, 8)
     others = [
         lax.ppermute(w, col_group, [(j, j ^ m) for j in range(4)]) for m in range(1, 4)
     ]
     w = jnp.stack([w] + others)
-    came = jnp.take(came, here ^ jnp.arange(16), axis=0, mode="clip")
-    came = jnp.transpose(came.reshape(16, pairs, rows, cols), (1, 3, 0, 2))
-    came = came.reshape(pairs, cols, block // 2)
-
-    sorted_slots = sort_slots(slot_block_table, layer_inputs, output_grads)
-    gathered = lax.all_to_all(sorted_slots, fsdp, split_axis=0, concat_axis=0, tiled=True)
-    gathered, w, came = lax.optimization_barrier((gathered, w, came))
-    right = spread(came, row_group, 8)
     partial = gram(gathered.reshape(-1, block))
     mine = lax.psum_scatter(partial, "z", scatter_dimension=0, tiled=True)
     mine = mine.reshape(2, rows, block)
@@ -257,7 +261,8 @@
     start = lax.axis_index(col_group) * 256 + lax.axis_index(row_group) * rows
     right_vals = lax.dynamic_slice(values_out, (pair % count_out, start), (pairs, rows))
     left_vals = lax.dynamic_index_in_dim(values_in, pair // count_out, 0, keepdims=False)
-    left_vals = jnp.transpose(left_vals.reshape(16, 2, rows), (1, 0, 2))
+    left_vals = jnp.take(left_vals.reshape(16, 2, rows), here ^ order, axis=0, mode="clip")
+    left_vals = jnp.transpose(left_vals, (1, 0, 2))
 
     rotated = rotate(lax.axis_index(col_group).reshape(1), w, right)
     slab = lax.all_to_all(rotated, row_group, split_axis=0, concat_axis=0, tiled=True)
@@ -267,10 +272,10 @@
     again = lax.all_to_all(back_rot, row_group, split_axis=0, concat_axis=0, tiled=True)
     parts = restore(again, right)
     parts = lax.all_to_all(parts, col_group, split_axis=0, concat_axis=0, tiled=True)
-    result = total(parts).astype(jnp.bfloat16).reshape(pairs, rows, 2, 16, rows)
-    result = jnp.transpose(result, (0, 1, 3, 2, 4)).reshape(pairs, rows, block)
-    preconditioned = lax.ppermute(result, axes, back_again)
-    return covariance, preconditioned
+    result = total(parts).astype(jnp.bfloat16)
+    result = lax.ppermute(result.reshape(pairs, rows, block), axes, back_again)
+    result = jnp.transpose(result.reshape(pairs, rows, 2, 16, rows), (0, 1, 3, 2, 4))
+    return covariance, result.reshape(pairs, rows, block)
 
 
 def solution(mesh):

time: 239 us -> 236 us (0.987)
  the two profiles are of different devices: /device:TPU:8 before, /device:TPU:66 now
where the time goes in v2:
time: 236 us; the launch traced here: 235 us
  starting transfers between devices  98.9 us (42%)
  waiting for transfers between devices  60.5 us (26%)
  blocking collectives  26.6 us (11%)
  local copies, waits for them, and re-layouts  19.5 us (8%)
  between operations  16.1 us (7%)
  Pallas kernels  12.2 us (5%)
    ppermute x3, starting transfers between devices, body(): lax.ppermute(w, col_group, [(j, j ^ m) for j in range(4)])  21.6 us
    ppermute x3, waiting for transfers between devices, body(): lax.ppermute(w, col_group, [(j, j ^ m) for j in range(4)])  20.7 us
    ppermute x3, starting transfers between devices, body(): lax.ppermute(pieces, 'z', [(i, i ^ m) for i in range(16)])  17 us
    all_to_all x1, blocking collectives, body(): lax.all_to_all(parts, col_group, split_axis=0, concat_axis=0, tiled=True)  16.3 us
    all_gather x1, waiting for transfers between devices, body(): left_t = lax.all_gather(moved[pairs], plane, axis=0, tiled=True)  14.5 us
    ppermute x1, starting transfers between devices, body(): lax.ppermute(jnp.concatenate([w, left_rows.reshape(1, rows, block)], axis...  13.8 us
    ppermute x1, waiting for transfers between devices, body(): result = lax.ppermute(result.reshape(pairs, rows, block), axes, back_again)  13.6 us
    ppermute x1, starting transfers between devices, body(): result = lax.ppermute(result.reshape(pairs, rows, block), axes, back_again)  11.7 us
  transfers between devices with their start and end apart: 17, of which 9 were waited for; matrix products, arithmetic and copies ran while one was open for 5% of the time, Pallas kernels for 5%

profile of v2, /device:TPU:66, one launch (start us, length us, event | category | flops | bytes accessed | tf_op | source)
XLA Modules:
  0.0 234.8 jit_solution(13096965094882832260)
XLA Ops:
  8.0 1.9 copy-done.2
  9.9 1.2 copy-done.4
  11.2 0.7 copy-done.5
  11.8 1.2 shard_map.95
  13.0 2.0 copy-done.1
  15.1 6.1 %all-to-all-start = ((bf16[16,128,1024]{2,1,0:T(8,128)(2,1)}), bf16[16,128,1024]{2,1,0:T(8,128)(2,1)}, u32[]{:S(2)}, u32[]{:S(2)}) async-start(bf16[16,128,1024]{2,1,0:T(8,128)(2,1)} %copy-done.1), calls=%async_computation | async-start | bytes 8388608 | tf_op jit(solution)/shard_map/all_to_all | solution.py:244
  21.4 3.8 %collective-permute-start.1 = (bf16[48,128]{1,0:T(8,128)(2,1)S(1)}, bf16[48,128]{1,0:T(8,128)(2,1)S(1)}, u32[]{:S(2)}, u32[]{:S(2)}) collective-permute-start(bf16[48,128]{1,0:T(8,128)(2,1)S(1)} %get-tuple-element.16), channel_id=1, source_target_pairs={{0,32},{32,0},{64,96},{96,64},{128,160},{160,128},{192,224},{224,1... | collective-permute-start | bytes 36872 | tf_op jit(solution)/shard_map/ppermute | solution.py:232
  25.3 3.9 %collective-permute-start.2 = (bf16[48,128]{1,0:T(8,128)(2,1)S(1)}, bf16[48,128]{1,0:T(8,128)(2,1)S(1)}, u32[]{:S(2)}, u32[]{:S(2)}) collective-permute-start(bf16[48,128]{1,0:T(8,128)(2,1)S(1)} %get-tuple-element.15), channel_id=1, source_target_pairs={{0,64},{32,96},{64,0},{96,32},{128,192},{160,224},{192,128},{224,1... | collective-permute-start | bytes 36872 | tf_op jit(solution)/shard_map/ppermute | solution.py:232
  29.2 2.5 %collective-permute-start.3 = (bf16[48,128]{1,0:T(8,128)(2,1)S(1)}, bf16[48,128]{1,0:T(8,128)(2,1)S(1)}, u32[]{:S(2)}, u32[]{:S(2)}) collective-permute-start(bf16[48,128]{1,0:T(8,128)(2,1)S(1)} %get-tuple-element.14), channel_id=1, source_target_pairs={{0,96},{32,64},{64,32},{96,0},{128,224},{160,192},{192,160},{224,1... | collective-permute-start | bytes 36872 | tf_op jit(solution)/shard_map/ppermute | solution.py:232
  32.0 0.6 gather_fusion
  33.2 0.6 reshape.69
  33.9 0.8 reshape.70
  34.8 13.8 %collective-permute-start = (bf16[4,32,1024]{2,1,0:T(8,128)(2,1)S(1)}, bf16[4,32,1024]{2,1,0:T(8,128)(2,1)S(1)}, u32[]{:S(2)}, u32[]{:S(2)}) collective-permute-start(bf16[4,32,1024]{2,1,0:T(8,128)(2,1)S(1)} %pad_maximum_fusion.1), channel_id=1, source_target_pairs={{0,0},{1,33},{2,66},{3,99},{4,132},{5,165},{6,198},{7,231},{8,264}... | collective-permute-start | bytes 786440 | tf_op jit(solution)/shard_map/ppermute | solution.py:222
  48.6 3.7 %collective-permute-start.4 = (bf16[4,48,128]{2,1,0:T(8,128)(2,1)S(1)}, bf16[4,48,128]{2,1,0:T(8,128)(2,1)S(1)}, u32[]{:S(2)}, u32[]{:S(2)}) collective-permute-start(bf16[4,48,128]{2,1,0:T(8,128)(2,1)S(1)} %pad_maximum_fusion.2), channel_id=1, source_target_pairs={{0,128},{32,160},{64,192},{96,224},{128,0},{160,32},{192,64},{224,... | collective-permute-start | bytes 147464 | tf_op jit(solution)/shard_map/ppermute | solution.py:234
  52.3 9.1 %collective-permute-start.5 = (bf16[4,48,128]{2,1,0:T(8,128)(2,1)S(1)}, bf16[4,48,128]{2,1,0:T(8,128)(2,1)S(1)}, u32[]{:S(2)}, u32[]{:S(2)}) collective-permute-start(bf16[4,48,128]{2,1,0:T(8,128)(2,1)S(1)} %pad_maximum_fusion.2), channel_id=1, source_target_pairs={{0,256},{32,288},{64,320},{96,352},{128,384},{160,416},{192,448},{... | collective-permute-start | bytes 147464 | tf_op jit(solution)/shard_map/ppermute | solution.py:234
  61.4 4.3 %collective-permute-start.6 = (bf16[4,48,128]{2,1,0:T(8,128)(2,1)S(1)}, bf16[4,48,128]{2,1,0:T(8,128)(2,1)S(1)}, u32[]{:S(2)}, u32[]{:S(2)}) collective-permute-start(bf16[4,48,128]{2,1,0:T(8,128)(2,1)S(1)} %pad_maximum_fusion.2), channel_id=1, source_target_pairs={{0,384},{32,416},{64,448},{96,480},{128,256},{160,288},{192,320},{... | collective-permute-start | bytes 147464 | tf_op jit(solution)/shard_map/ppermute | solution.py:234
  65.7 2.5 %collective-permute-done.4 = bf16[4,48,128]{2,1,0:T(8,128)(2,1)S(1)} collective-permute-done((bf16[4,48,128]{2,1,0:T(8,128)(2,1)S(1)}, bf16[4,48,128]{2,1,0:T(8,128)(2,1)S(1)}, u32[]{:S(2)}, u32[]{:S(2)}) %collective-permute-start.4) | collective-permute-done | bytes 49184 | tf_op jit(solution)/shard_map/ppermute | solution.py:234
  68.7 3.1 %collective-permute-done.6 = bf16[4,48,128]{2,1,0:T(8,128)(2,1)S(1)} collective-permute-done((bf16[4,48,128]{2,1,0:T(8,128)(2,1)S(1)}, bf16[4,48,128]{2,1,0:T(8,128)(2,1)S(1)}, u32[]{:S(2)}, u32[]{:S(2)}) %collective-permute-start.6) | collective-permute-done | bytes 49184 | tf_op jit(solution)/shard_map/ppermute | solution.py:234
  71.8 0.6 slice.7
  72.6 0.6 gather_fusion.1
  73.4 5.6 %all-to-all-done = bf16[16,128,1024]{2,1,0:T(8,128)(2,1)} async-done(((bf16[16,128,1024]{2,1,0:T(8,128)(2,1)}), bf16[16,128,1024]{2,1,0:T(8,128)(2,1)}, u32[]{:S(2)}, u32[]{:S(2)}) %all-to-all-start) | async-done | bytes 4194336 | tf_op jit(solution)/shard_map/all_to_all | solution.py:244
  79.0 8.3 %shard_map.96 = bf16[1024,1024]{1,0:T(8,128)(2,1)} custom-call(bf16[2048,1024]{1,0:T(8,128)(2,1)} %bitcast.12.x), custom_call_target="tpu_custom_call" | custom-call | flops 4294967296 | bytes 6291456 | tf_op jit(solution)/shard_map/pallas_call | solution.py:100
  87.4 1.3 broadcast_in_dim.7
  88.7 11.5 %all-to-all-start.1 = ((bf16[8,3,64,512]{3,2,1,0:T(8,128)(2,1)}), bf16[8,3,64,512]{3,2,1,0:T(8,128)(2,1)S(1)}, u32[]{:S(2)}, u32[]{:S(2)}) async-start(bf16[8,3,64,512]{3,2,1,0:T(8,128)(2,1)} %broadcast_in_dim.7), calls=%async_computation.2 | async-start | bytes 3145728 | tf_op jit(solution)/shard_map/all_to_all | solution.py:185
  100.2 12.8 %collective-permute-start.10 = (bf16[3,32,1024]{2,1,0:T(8,128)(2,1)S(1)}, bf16[3,32,1024]{2,1,0:T(8,128)(2,1)S(1)}, u32[]{:S(2)}, u32[]{:S(2)}) collective-permute-start(bf16[3,32,1024]{2,1,0:T(8,128)(2,1)S(1)} %slice.6), channel_id=1, source_target_pairs={{0,12},{4,8},{8,4},{12,0},{1,13},{5,9},{9,5},{13,1},{2,14},{6,10},... | collective-permute-start | bytes 589832 | tf_op jit(solution)/shard_map/ppermute | solution.py:248
  113.1 6.9 %collective-permute-start.9 = (bf16[3,32,1024]{2,1,0:T(8,128)(2,1)S(1)}, bf16[3,32,1024]{2,1,0:T(8,128)(2,1)S(1)}, u32[]{:S(2)}, u32[]{:S(2)}) collective-permute-start(bf16[3,32,1024]{2,1,0:T(8,128)(2,1)S(1)} %slice.6), channel_id=1, source_target_pairs={{0,8},{4,12},{8,0},{12,4},{1,9},{5,13},{9,1},{13,5},{2,10},{6,14},... | collective-permute-start | bytes 589832 | tf_op jit(solution)/shard_map/ppermute | solution.py:248
  119.9 1.9 collective-permute-start.8
  121.9 13.5 %collective-permute-done.10 = bf16[3,32,1024]{2,1,0:T(8,128)(2,1)S(1)} collective-permute-done((bf16[3,32,1024]{2,1,0:T(8,128)(2,1)S(1)}, bf16[3,32,1024]{2,1,0:T(8,128)(2,1)S(1)}, u32[]{:S(2)}, u32[]{:S(2)}) %collective-permute-start.10) | collective-permute-done | bytes 196640 | tf_op jit(solution)/shard_map/ppermute | solution.py:248
  135.3 4.5 %collective-permute-done.9 = bf16[3,32,1024]{2,1,0:T(8,128)(2,1)S(1)} collective-permute-done((bf16[3,32,1024]{2,1,0:T(8,128)(2,1)S(1)}, bf16[3,32,1024]{2,1,0:T(8,128)(2,1)S(1)}, u32[]{:S(2)}, u32[]{:S(2)}) %collective-permute-start.9) | collective-permute-done | bytes 196640 | tf_op jit(solution)/shard_map/ppermute | solution.py:248
  139.9 2.7 %collective-permute-done.8 = bf16[3,32,1024]{2,1,0:T(8,128)(2,1)S(1)} collective-permute-done((bf16[3,32,1024]{2,1,0:T(8,128)(2,1)S(1)}, bf16[3,32,1024]{2,1,0:T(8,128)(2,1)S(1)}, u32[]{:S(2)}, u32[]{:S(2)}) %collective-permute-start.8) | collective-permute-done | bytes 196640 | tf_op jit(solution)/shard_map/ppermute | solution.py:248
  142.7 1.2 shard_map.97
  143.9 4.7 %all-to-all-start.2 = ((bf16[8,3,32,128]{3,2,1,0:T(8,128)(2,1)}), bf16[8,3,32,128]{3,2,1,0:T(8,128)(2,1)S(1)}, u32[]{:S(2)}, u32[]{:S(2)}) async-start(bf16[8,3,32,128]{3,2,1,0:T(8,128)(2,1)} %shard_map.97), calls=%async_computation.3 | async-start | bytes 393216 | tf_op jit(solution)/shard_map/all_to_all | solution.py:268
  148.7 0.7 dynamic-slice_reduce_fusion
  149.5 0.6 gather_fusion.2
  150.2 0.8 dynamic_slice.39
  151.1 14.5 %all-gather.3.cloned.1.call-done = bf16[1,1024,1024]{2,1,0:T(8,128)(2,1)} async-done(((bf16[1,32,1024]{2,1,0:T(8,128)(2,1)}), bf16[1,1024,1024]{2,1,0:T(8,128)(2,1)}) %all-gather.3.cloned.1.call-update) | async-done | bytes 2097168 | tf_op jit(solution)/shard_map/all_gather | solution.py:238
  165.6 1.6 copy-done.3
  167.2 1.1 shard_map.98
  168.3 10.3 %all_to_all.25.x = bf16[8,3,32,128]{3,2,1,0:T(8,128)(2,1)S(1)} all-to-all(bf16[8,3,32,128]{3,2,1,0:T(8,128)(2,1)S(1)} %shard_map.98), channel_id=1, replica_groups=mesh['z'=16,'xh'=2,'xl'=2,'yh'=2,'yl'=2,'c'=2] {'xh','yl','c'}, dimensions={0} | all-to-all | bytes 393216 | tf_op jit(solution)/shard_map/all_to_all | solution.py:272
  179.0 16.3 %all_to_all.26 = bf16[4,3,32,1024]{3,2,1,0:T(8,128)(2,1)S(1)} all-to-all(bf16[4,3,32,1024]{3,2,1,0:T(8,128)(2,1)S(1)} %shard_map.99), channel_id=1, replica_groups=mesh['z'=16,'xh'=2,'xl'=2,'yh'=2,'yl'=2,'c'=2] {'xl','yh'}, dimensions={0} | all-to-all | bytes 1572864 | tf_op jit(solution)/shard_map/all_to_all | solution.py:274
  195.5 11.7 %collective-permute-start.11 = (bf16[3,32,1024]{2,1,0:T(8,128)(2,1)S(1)}, bf16[3,32,1024]{2,1,0:T(8,128)(2,1)S(1)}, u32[]{:S(2)}, u32[]{:S(2)}) collective-permute-start(bf16[3,32,1024]{2,1,0:T(8,128)(2,1)S(1)} %reduce_sum.12), channel_id=1, source_target_pairs={{0,0},{33,1},{66,2},{99,3},{132,4},{165,5},{198,6},{231,7},{264,8}... | collective-permute-start | bytes 589832 | tf_op jit(solution)/shard_map/ppermute | solution.py:276
  207.2 0.9 constant_dynamic-slice_fusion
  208.1 2.1 collective-permute-start.7
  210.3 13.6 %collective-permute-done.11 = bf16[3,32,1024]{2,1,0:T(8,128)(2,1)S(1)} collective-permute-done((bf16[3,32,1024]{2,1,0:T(8,128)(2,1)S(1)}, bf16[3,32,1024]{2,1,0:T(8,128)(2,1)S(1)}, u32[]{:S(2)}, u32[]{:S(2)}) %collective-permute-start.11) | collective-permute-done | bytes 196640 | tf_op jit(solution)/shard_map/ppermute | solution.py:276
  223.9 0.6 reshape.83
  224.5 0.7 copy.25
  225.1 1.5 reshape.84
  226.6 0.7 add_multiply_fusion
  (57 shorter events, 3.1 us)
Async XLA Ops:
  8.0 23.8 %copy-start = (bf16[4,1024,32]{1,2,0:T(8,128)(2,1)S(1)}, bf16[4,1024,32]{1,2,0:T(8,128)(2,1)}, u32[]{:S(2)}) copy-start(bf16[4,1024,32]{1,2,0:T(8,128)(2,1)} %param.12) | copy-start | bytes 786436
  8.0 1.9 copy-start.2
  9.9 1.2 copy-start.4
  11.2 0.7 copy-start.5
  13.0 2.0 copy-start.1
  15.1 6.2 %copy-start.8 = (bf16[12,32,64]{2,1,0:T(8,128)(2,1)S(1)}, bf16[12,32,64]{2,1,0:T(8,128)(2,1)}, u32[]{:S(2)}) copy-start(bf16[12,32,64]{2,1,0:T(8,128)(2,1)} %param.13) | copy-start | bytes 147460
  15.1 63.9 %all-to-all-start = ((bf16[16,128,1024]{2,1,0:T(8,128)(2,1)}), bf16[16,128,1024]{2,1,0:T(8,128)(2,1)}, u32[]{:S(2)}, u32[]{:S(2)}) async-start(bf16[16,128,1024]{2,1,0:T(8,128)(2,1)} %copy-done.1), calls=%async_computation | async-start | bytes 8388608 | tf_op jit(solution)/shard_map/all_to_all | solution.py:244
  21.1 12.1 %copy-start.6 = (bf16[3,32,1024]{2,1,0:T(8,128)(2,1)S(1)}, bf16[3,32,1024]{2,1,0:T(8,128)(2,1)}, u32[]{:S(2)}) copy-start(bf16[3,32,1024]{2,1,0:T(8,128)(2,1)} %param.11) | copy-start | bytes 589828
  21.2 144.4 %all-gather.3.cloned.1.call-start = ((), (), s32[]{:S(2)}) async-start(), calls=%async_computation.7 | async-start | bytes 2162688 | tf_op jit(solution)/shard_map/all_gather | solution.py:238
  21.4 27.1 %collective-permute-start.1 = (bf16[48,128]{1,0:T(8,128)(2,1)S(1)}, bf16[48,128]{1,0:T(8,128)(2,1)S(1)}, u32[]{:S(2)}, u32[]{:S(2)}) collective-permute-start(bf16[48,128]{1,0:T(8,128)(2,1)S(1)} %get-tuple-element.16), channel_id=1, source_target_pairs={{0,32},{32,0},{64,96},{96,64},{128,160},{160,128},{192,224},{224,1... | collective-permute-start | bytes 36872 | tf_op jit(solution)/shard_map/ppermute | solution.py:232
  25.3 23.3 %collective-permute-start.2 = (bf16[48,128]{1,0:T(8,128)(2,1)S(1)}, bf16[48,128]{1,0:T(8,128)(2,1)S(1)}, u32[]{:S(2)}, u32[]{:S(2)}) collective-permute-start(bf16[48,128]{1,0:T(8,128)(2,1)S(1)} %get-tuple-element.15), channel_id=1, source_target_pairs={{0,64},{32,96},{64,0},{96,32},{128,192},{160,224},{192,128},{224,1... | collective-permute-start | bytes 36872 | tf_op jit(solution)/shard_map/ppermute | solution.py:232
  29.2 19.4 %collective-permute-start.3 = (bf16[48,128]{1,0:T(8,128)(2,1)S(1)}, bf16[48,128]{1,0:T(8,128)(2,1)S(1)}, u32[]{:S(2)}, u32[]{:S(2)}) collective-permute-start(bf16[48,128]{1,0:T(8,128)(2,1)S(1)} %get-tuple-element.14), channel_id=1, source_target_pairs={{0,96},{32,64},{64,32},{96,0},{128,224},{160,192},{192,160},{224,1... | collective-permute-start | bytes 36872 | tf_op jit(solution)/shard_map/ppermute | solution.py:232
  34.8 37.1 %collective-permute-start = (bf16[4,32,1024]{2,1,0:T(8,128)(2,1)S(1)}, bf16[4,32,1024]{2,1,0:T(8,128)(2,1)S(1)}, u32[]{:S(2)}, u32[]{:S(2)}) collective-permute-start(bf16[4,32,1024]{2,1,0:T(8,128)(2,1)S(1)} %pad_maximum_fusion.1), channel_id=1, source_target_pairs={{0,0},{1,33},{2,66},{3,99},{4,132},{5,165},{6,198},{7,231},{8,264}... | collective-permute-start | bytes 786440 | tf_op jit(solution)/shard_map/ppermute | solution.py:222
  48.6 19.6 %collective-permute-start.4 = (bf16[4,48,128]{2,1,0:T(8,128)(2,1)S(1)}, bf16[4,48,128]{2,1,0:T(8,128)(2,1)S(1)}, u32[]{:S(2)}, u32[]{:S(2)}) collective-permute-start(bf16[4,48,128]{2,1,0:T(8,128)(2,1)S(1)} %pad_maximum_fusion.2), channel_id=1, source_target_pairs={{0,128},{32,160},{64,192},{96,224},{128,0},{160,32},{192,64},{224,... | collective-permute-start | bytes 147464 | tf_op jit(solution)/shard_map/ppermute | solution.py:234
  52.3 16.4 %collective-permute-start.5 = (bf16[4,48,128]{2,1,0:T(8,128)(2,1)S(1)}, bf16[4,48,128]{2,1,0:T(8,128)(2,1)S(1)}, u32[]{:S(2)}, u32[]{:S(2)}) collective-permute-start(bf16[4,48,128]{2,1,0:T(8,128)(2,1)S(1)} %pad_maximum_fusion.2), channel_id=1, source_target_pairs={{0,256},{32,288},{64,320},{96,352},{128,384},{160,416},{192,448},{... | collective-permute-start | bytes 147464 | tf_op jit(solution)/shard_map/ppermute | solution.py:234
  61.4 10.4 %collective-permute-start.6 = (bf16[4,48,128]{2,1,0:T(8,128)(2,1)S(1)}, bf16[4,48,128]{2,1,0:T(8,128)(2,1)S(1)}, u32[]{:S(2)}, u32[]{:S(2)}) collective-permute-start(bf16[4,48,128]{2,1,0:T(8,128)(2,1)S(1)} %pad_maximum_fusion.2), channel_id=1, source_target_pairs={{0,384},{32,416},{64,448},{96,480},{128,256},{160,288},{192,320},{... | collective-permute-start | bytes 147464 | tf_op jit(solution)/shard_map/ppermute | solution.py:234
  72.5 134.7 %reduce-scatter.2.cloned.1.call-start = ((), (), s32[]{:S(2)}) async-start(), calls=%async_computation.6 | async-start | bytes 2228224 | tf_op jit(solution)/shard_map/reduce_scatter | solution.py:252
  88.7 53.9 %all-to-all-start.1 = ((bf16[8,3,64,512]{3,2,1,0:T(8,128)(2,1)}), bf16[8,3,64,512]{3,2,1,0:T(8,128)(2,1)S(1)}, u32[]{:S(2)}, u32[]{:S(2)}) async-start(bf16[8,3,64,512]{3,2,1,0:T(8,128)(2,1)} %broadcast_in_dim.7), calls=%async_computation.2 | async-start | bytes 3145728 | tf_op jit(solution)/shard_map/all_to_all | solution.py:185
  100.2 35.1 %collective-permute-start.10 = (bf16[3,32,1024]{2,1,0:T(8,128)(2,1)S(1)}, bf16[3,32,1024]{2,1,0:T(8,128)(2,1)S(1)}, u32[]{:S(2)}, u32[]{:S(2)}) collective-permute-start(bf16[3,32,1024]{2,1,0:T(8,128)(2,1)S(1)} %slice.6), channel_id=1, source_target_pairs={{0,12},{4,8},{8,4},{12,0},{1,13},{5,9},{9,5},{13,1},{2,14},{6,10},... | collective-permute-start | bytes 589832 | tf_op jit(solution)/shard_map/ppermute | solution.py:248
  113.1 26.8 %collective-permute-start.9 = (bf16[3,32,1024]{2,1,0:T(8,128)(2,1)S(1)}, bf16[3,32,1024]{2,1,0:T(8,128)(2,1)S(1)}, u32[]{:S(2)}, u32[]{:S(2)}) collective-permute-start(bf16[3,32,1024]{2,1,0:T(8,128)(2,1)S(1)} %slice.6), channel_id=1, source_target_pairs={{0,8},{4,12},{8,0},{12,4},{1,9},{5,13},{9,1},{13,5},{2,10},{6,14},... | collective-permute-start | bytes 589832 | tf_op jit(solution)/shard_map/ppermute | solution.py:248
  119.9 22.6 %collective-permute-start.8 = (bf16[3,32,1024]{2,1,0:T(8,128)(2,1)S(1)}, bf16[3,32,1024]{2,1,0:T(8,128)(2,1)S(1)}, u32[]{:S(2)}, u32[]{:S(2)}) collective-permute-start(bf16[3,32,1024]{2,1,0:T(8,128)(2,1)S(1)} %slice.6), channel_id=1, source_target_pairs={{0,4},{4,0},{8,12},{12,8},{1,5},{5,1},{9,13},{13,9},{2,6},{6,2},{1... | collective-permute-start | bytes 589832 | tf_op jit(solution)/shard_map/ppermute | solution.py:248
  143.9 21.7 %all-to-all-start.2 = ((bf16[8,3,32,128]{3,2,1,0:T(8,128)(2,1)}), bf16[8,3,32,128]{3,2,1,0:T(8,128)(2,1)S(1)}, u32[]{:S(2)}, u32[]{:S(2)}) async-start(bf16[8,3,32,128]{3,2,1,0:T(8,128)(2,1)} %shard_map.97), calls=%async_computation.3 | async-start | bytes 393216 | tf_op jit(solution)/shard_map/all_to_all | solution.py:268
  165.6 1.6 copy-start.3
  195.5 28.4 %collective-permute-start.11 = (bf16[3,32,1024]{2,1,0:T(8,128)(2,1)S(1)}, bf16[3,32,1024]{2,1,0:T(8,128)(2,1)S(1)}, u32[]{:S(2)}, u32[]{:S(2)}) collective-permute-start(bf16[3,32,1024]{2,1,0:T(8,128)(2,1)S(1)} %reduce_sum.12), channel_id=1, source_target_pairs={{0,0},{33,1},{66,2},{99,3},{132,4},{165,5},{198,6},{231,7},{264,8}... | collective-permute-start | bytes 589832 | tf_op jit(solution)/shard_map/ppermute | solution.py:276
  207.2 19.4 %copy-start.7 = (bf16[64,1024]{1,0:T(8,128)(2,1)S(1)}, bf16[64,1024]{1,0:T(8,128)(2,1)}, u32[]{:S(2)}) copy-start(bf16[64,1024]{1,0:T(8,128)(2,1)} %reduce-scatter.2.cloned.1.call-done) | copy-start | bytes 393220
  208.1 18.5 %collective-permute-start.7 = (bf16[1,32,1024]{2,1,0:T(8,128)(2,1)S(1)}, bf16[1,32,1024]{2,1,0:T(8,128)(2,1)S(1)}, u32[]{:S(2)}, u32[]{:S(2)}) collective-permute-start(bf16[1,32,1024]{2,1,0:T(8,128)(2,1)S(1)} %constant_dynamic-slice_fusion), channel_id=1, source_target_pairs={{0,16},{16,0},{1,17},{17,1},{2,18},{18,2},{3,19},{19,3},{4,20},{20... | collective-permute-start | bytes 196616 | tf_op jit(solution)/shard_map/ppermute | solution.py:257
Sparse Core Ops, SparseCore 0:
  72.6 92.9 all-gather.2
Sparse Core Ops, SparseCore 1:
  87.3 92.5 reduce-scatter.1

commit v3 on v2

--- a/solution.py
+++ b/solution.py
@@ -231,11 +231,11 @@
         piece = lax.dynamic_index_in_dim(wanted, (here ^ m) % groups, 0, keepdims=False)
         pieces.append(lax.ppermute(piece, "z", [(i, i ^ m) for i in range(16)]) if m else piece)
     pieces = jnp.stack(pieces)
+    moved, _ = lax.optimization_barrier((moved, pieces))
+    w = moved[:pairs]
+    left_t = lax.all_gather(moved[pairs], plane, axis=0, tiled=True)
     far = [lax.ppermute(pieces, "z", [(i, i ^ m) for i in range(16)]) for m in (4, 8, 12)]
     came = jnp.concatenate([pieces] + far)
-    moved, came = lax.optimization_barrier((moved, came))
-    w = moved[:pairs]
-    left_t = lax.all_gather(moved[pairs], plane, axis=0, tiled=True)
     came = jnp.take(came, here ^ order, axis=0, mode="clip")
     came = jnp.transpose(came.reshape(16, pairs, rows, cols), (1, 3, 0, 2))
     came = came.reshape(pairs, cols, block // 2)

time: 236 us -> 256 us (1.085)
  the two profiles are of different devices: /device:TPU:66 before, /device:TPU:34 now
where the time goes in v3:
time: 256 us; the launch traced here: 255 us
  starting transfers between devices  122 us (48%)
  waiting for transfers between devices  58.3 us (23%)
  blocking collectives  25.6 us (10%)
  local copies, waits for them, and re-layouts  19.4 us (8%)
  between operations  16.1 us (6%)
  Pallas kernels  12.2 us (5%)
    ppermute x3, starting transfers between devices, body(): lax.ppermute(pieces, 'z', [(i, i ^ m) for i in range(16)])  38.1 us
    ppermute x3, waiting for transfers between devices, body(): lax.ppermute(w, col_group, [(j, j ^ m) for j in range(4)])  23.3 us
    ppermute x3, starting transfers between devices, body(): lax.ppermute(w, col_group, [(j, j ^ m) for j in range(4)])  21.6 us
    all_to_all x1, starting transfers between devices, spread(): lax.all_to_all(copies, names, split_axis=0, concat_axis=0, tiled=True)  20.3 us
    ppermute x1, waiting for transfers between devices, body(): result = lax.ppermute(result.reshape(pairs, rows, block), axes, back_again)  19.2 us
    all_to_all x1, blocking collectives, body(): lax.all_to_all(parts, col_group, split_axis=0, concat_axis=0, tiled=True)  16.1 us
    ppermute x1, starting transfers between devices, body(): lax.ppermute(jnp.concatenate([w, left_rows.reshape(1, rows, block)], axis...  14.1 us
    ppermute x3, starting transfers between devices, body(): lax.ppermute(piece, 'z', [(i, i ^ m) for i in range(16)])  9.81 us
  transfers between devices with their start and end apart: 17, of which 7 were waited for; matrix products, arithmetic and copies ran while one was open for 5% of the time, Pallas kernels for 4%

profile of v3, /device:TPU:34, one launch (start us, length us, event | category | flops | bytes accessed | tf_op | source)
XLA Modules:
  0.0 254.8 jit_solution(8135425350609085007)
XLA Ops:
  8.0 1.9 copy-done.2
  9.9 1.2 copy-done.4
  11.2 0.7 copy-done.5
  11.8 1.2 shard_map.95
  13.0 2.0 copy-done.1
  15.0 5.9 %all-to-all-start = ((bf16[16,128,1024]{2,1,0:T(8,128)(2,1)}), bf16[16,128,1024]{2,1,0:T(8,128)(2,1)}, u32[]{:S(2)}, u32[]{:S(2)}) async-start(bf16[16,128,1024]{2,1,0:T(8,128)(2,1)} %copy-done.1), calls=%async_computation | async-start | bytes 8388608 | tf_op jit(solution)/shard_map/all_to_all | solution.py:244
  21.3 0.6 gather_fusion
  22.3 0.3 reshape.73
  22.6 0.6 reshape.69
  23.3 0.8 reshape.70
  24.1 14.1 %collective-permute-start = (bf16[4,32,1024]{2,1,0:T(8,128)(2,1)S(1)}, bf16[4,32,1024]{2,1,0:T(8,128)(2,1)S(1)}, u32[]{:S(2)}, u32[]{:S(2)}) collective-permute-start(bf16[4,32,1024]{2,1,0:T(8,128)(2,1)S(1)} %pad_maximum_fusion.1), channel_id=1, source_target_pairs={{0,0},{1,33},{2,66},{3,99},{4,132},{5,165},{6,198},{7,231},{8,264}... | collective-permute-start | bytes 786440 | tf_op jit(solution)/shard_map/ppermute | solution.py:222
  38.5 3.6 %collective-permute-start.3 = (bf16[48,128]{1,0:T(8,128)(2,1)S(1)}, bf16[48,128]{1,0:T(8,128)(2,1)S(1)}, u32[]{:S(2)}, u32[]{:S(2)}) collective-permute-start(bf16[48,128]{1,0:T(8,128)(2,1)S(1)} %get-tuple-element.12), channel_id=1, source_target_pairs={{0,96},{32,64},{64,32},{96,0},{128,224},{160,192},{192,160},{224,1... | collective-permute-start | bytes 36872 | tf_op jit(solution)/shard_map/ppermute | solution.py:232
  42.1 4.3 %collective-permute-start.2 = (bf16[48,128]{1,0:T(8,128)(2,1)S(1)}, bf16[48,128]{1,0:T(8,128)(2,1)S(1)}, u32[]{:S(2)}, u32[]{:S(2)}) collective-permute-start(bf16[48,128]{1,0:T(8,128)(2,1)S(1)} %get-tuple-element.13), channel_id=1, source_target_pairs={{0,64},{32,96},{64,0},{96,32},{128,192},{160,224},{192,128},{224,1... | collective-permute-start | bytes 36872 | tf_op jit(solution)/shard_map/ppermute | solution.py:232
  46.4 1.9 collective-permute-start.1
  48.6 3.4 %collective-permute-done.1 = bf16[48,128]{1,0:T(8,128)(2,1)S(1)} collective-permute-done((bf16[48,128]{1,0:T(8,128)(2,1)S(1)}, bf16[48,128]{1,0:T(8,128)(2,1)S(1)}, u32[]{:S(2)}, u32[]{:S(2)}) %collective-permute-start.1) | collective-permute-done | bytes 12320 | tf_op jit(solution)/shard_map/ppermute | solution.py:232
  52.0 0.6 slice.7
  52.8 21.3 %collective-permute-start.4 = (bf16[4,48,128]{2,1,0:T(8,128)(2,1)S(1)}, bf16[4,48,128]{2,1,0:T(8,128)(2,1)S(1)}, u32[]{:S(2)}, u32[]{:S(2)}) collective-permute-start(bf16[4,48,128]{2,1,0:T(8,128)(2,1)S(1)} %pad_maximum_fusion.2), channel_id=1, source_target_pairs={{0,128},{32,160},{64,192},{96,224},{128,0},{160,32},{192,64},{224,... | collective-permute-start | bytes 147464 | tf_op jit(solution)/shard_map/ppermute | solution.py:237
  74.0 14.4 %collective-permute-start.5 = (bf16[4,48,128]{2,1,0:T(8,128)(2,1)S(1)}, bf16[4,48,128]{2,1,0:T(8,128)(2,1)S(1)}, u32[]{:S(2)}, u32[]{:S(2)}) collective-permute-start(bf16[4,48,128]{2,1,0:T(8,128)(2,1)S(1)} %pad_maximum_fusion.2), channel_id=1, source_target_pairs={{0,256},{32,288},{64,320},{96,352},{128,384},{160,416},{192,448},{... | collective-permute-start | bytes 147464 | tf_op jit(solution)/shard_map/ppermute | solution.py:237
  88.4 2.5 collective-permute-start.6
  91.0 7.3 %collective-permute-done.6 = bf16[4,48,128]{2,1,0:T(8,128)(2,1)S(1)} collective-permute-done((bf16[4,48,128]{2,1,0:T(8,128)(2,1)S(1)}, bf16[4,48,128]{2,1,0:T(8,128)(2,1)S(1)}, u32[]{:S(2)}, u32[]{:S(2)}) %collective-permute-start.6) | collective-permute-done | bytes 49184 | tf_op jit(solution)/shard_map/ppermute | solution.py:237
  98.3 0.6 gather_fusion.1
  99.1 8.3 %shard_map.96 = bf16[1024,1024]{1,0:T(8,128)(2,1)} custom-call(bf16[2048,1024]{1,0:T(8,128)(2,1)} %bitcast.12.x), custom_call_target="tpu_custom_call" | custom-call | flops 4294967296 | bytes 6291456 | tf_op jit(solution)/shard_map/pallas_call | solution.py:100
  107.6 1.3 broadcast_in_dim.7
  108.9 20.3 %all-to-all-start.1 = ((bf16[8,3,64,512]{3,2,1,0:T(8,128)(2,1)}), bf16[8,3,64,512]{3,2,1,0:T(8,128)(2,1)S(1)}, u32[]{:S(2)}, u32[]{:S(2)}) async-start(bf16[8,3,64,512]{3,2,1,0:T(8,128)(2,1)} %broadcast_in_dim.7), calls=%async_computation.2 | async-start | bytes 3145728 | tf_op jit(solution)/shard_map/all_to_all | solution.py:185
  129.3 1.9 collective-permute-start.10
  131.2 14.9 %collective-permute-start.9 = (bf16[3,32,1024]{2,1,0:T(8,128)(2,1)S(1)}, bf16[3,32,1024]{2,1,0:T(8,128)(2,1)S(1)}, u32[]{:S(2)}, u32[]{:S(2)}) collective-permute-start(bf16[3,32,1024]{2,1,0:T(8,128)(2,1)S(1)} %slice.6), channel_id=1, source_target_pairs={{0,8},{4,12},{8,0},{12,4},{1,9},{5,13},{9,1},{13,5},{2,10},{6,14},... | collective-permute-start | bytes 589832 | tf_op jit(solution)/shard_map/ppermute | solution.py:248
  146.0 4.9 %collective-permute-start.8 = (bf16[3,32,1024]{2,1,0:T(8,128)(2,1)S(1)}, bf16[3,32,1024]{2,1,0:T(8,128)(2,1)S(1)}, u32[]{:S(2)}, u32[]{:S(2)}) collective-permute-start(bf16[3,32,1024]{2,1,0:T(8,128)(2,1)S(1)} %slice.6), channel_id=1, source_target_pairs={{0,4},{4,0},{8,12},{12,8},{1,5},{5,1},{9,13},{13,9},{2,6},{6,2},{1... | collective-permute-start | bytes 589832 | tf_op jit(solution)/shard_map/ppermute | solution.py:248
  150.9 4.7 %collective-permute-done.10 = bf16[3,32,1024]{2,1,0:T(8,128)(2,1)S(1)} collective-permute-done((bf16[3,32,1024]{2,1,0:T(8,128)(2,1)S(1)}, bf16[3,32,1024]{2,1,0:T(8,128)(2,1)S(1)}, u32[]{:S(2)}, u32[]{:S(2)}) %collective-permute-start.10) | collective-permute-done | bytes 196640 | tf_op jit(solution)/shard_map/ppermute | solution.py:248
  155.7 18.6 %collective-permute-done.9 = bf16[3,32,1024]{2,1,0:T(8,128)(2,1)S(1)} collective-permute-done((bf16[3,32,1024]{2,1,0:T(8,128)(2,1)S(1)}, bf16[3,32,1024]{2,1,0:T(8,128)(2,1)S(1)}, u32[]{:S(2)}, u32[]{:S(2)}) %collective-permute-start.9) | collective-permute-done | bytes 196640 | tf_op jit(solution)/shard_map/ppermute | solution.py:248
  174.4 1.3 shard_map.97
  175.6 5.0 %all-to-all-start.2 = ((bf16[8,3,32,128]{3,2,1,0:T(8,128)(2,1)}), bf16[8,3,32,128]{3,2,1,0:T(8,128)(2,1)S(1)}, u32[]{:S(2)}, u32[]{:S(2)}) async-start(bf16[8,3,32,128]{3,2,1,0:T(8,128)(2,1)} %shard_map.97), calls=%async_computation.3 | async-start | bytes 393216 | tf_op jit(solution)/shard_map/all_to_all | solution.py:268
  180.6 0.7 dynamic-slice_reduce_fusion
  181.4 0.6 gather_fusion.2
  182.1 0.8 dynamic_slice.39
  183.0 4.7 %all-to-all-done.2.x = bf16[8,3,32,128]{3,2,1,0:T(8,128)(2,1)S(1)} async-done(((bf16[8,3,32,128]{3,2,1,0:T(8,128)(2,1)}), bf16[8,3,32,128]{3,2,1,0:T(8,128)(2,1)S(1)}, u32[]{:S(2)}, u32[]{:S(2)}) %all-to-all-start.2) | async-done | bytes 196640 | tf_op jit(solution)/shard_map/all_to_all | solution.py:268
  187.8 1.6 copy-done.3
  189.3 1.1 shard_map.98
  190.5 9.6 %all_to_all.25.x = bf16[8,3,32,128]{3,2,1,0:T(8,128)(2,1)S(1)} all-to-all(bf16[8,3,32,128]{3,2,1,0:T(8,128)(2,1)S(1)} %shard_map.98), channel_id=1, replica_groups=mesh['z'=16,'xh'=2,'xl'=2,'yh'=2,'yl'=2,'c'=2] {'xh','yl','c'}, dimensions={0} | all-to-all | bytes 393216 | tf_op jit(solution)/shard_map/all_to_all | solution.py:272
  200.0 0.4 shard_map.99
  200.4 16.1 %all_to_all.26 = bf16[4,3,32,1024]{3,2,1,0:T(8,128)(2,1)S(1)} all-to-all(bf16[4,3,32,1024]{3,2,1,0:T(8,128)(2,1)S(1)} %shard_map.99), channel_id=1, replica_groups=mesh['z'=16,'xh'=2,'xl'=2,'yh'=2,'yl'=2,'c'=2] {'xl','yh'}, dimensions={0} | all-to-all | bytes 1572864 | tf_op jit(solution)/shard_map/all_to_all | solution.py:274
  216.7 4.1 %collective-permute-start.11 = (bf16[3,32,1024]{2,1,0:T(8,128)(2,1)S(1)}, bf16[3,32,1024]{2,1,0:T(8,128)(2,1)S(1)}, u32[]{:S(2)}, u32[]{:S(2)}) collective-permute-start(bf16[3,32,1024]{2,1,0:T(8,128)(2,1)S(1)} %reduce_sum.12), channel_id=1, source_target_pairs={{0,0},{33,1},{66,2},{99,3},{132,4},{165,5},{198,6},{231,7},{264,8}... | collective-permute-start | bytes 589832 | tf_op jit(solution)/shard_map/ppermute | solution.py:276
  220.8 0.9 constant_dynamic-slice_fusion
  221.8 3.0 %collective-permute-start.7 = (bf16[1,32,1024]{2,1,0:T(8,128)(2,1)S(1)}, bf16[1,32,1024]{2,1,0:T(8,128)(2,1)S(1)}, u32[]{:S(2)}, u32[]{:S(2)}) collective-permute-start(bf16[1,32,1024]{2,1,0:T(8,128)(2,1)S(1)} %constant_dynamic-slice_fusion), channel_id=1, source_target_pairs={{0,16},{16,0},{1,17},{17,1},{2,18},{18,2},{3,19},{19,3},{4,20},{20... | collective-permute-start | bytes 196616 | tf_op jit(solution)/shard_map/ppermute | solution.py:257
  224.8 19.2 %collective-permute-done.11 = bf16[3,32,1024]{2,1,0:T(8,128)(2,1)S(1)} collective-permute-done((bf16[3,32,1024]{2,1,0:T(8,128)(2,1)S(1)}, bf16[3,32,1024]{2,1,0:T(8,128)(2,1)S(1)}, u32[]{:S(2)}, u32[]{:S(2)}) %collective-permute-start.11) | collective-permute-done | bytes 196640 | tf_op jit(solution)/shard_map/ppermute | solution.py:276
  244.0 0.6 reshape.83
  244.5 0.7 copy.25
  245.2 1.5 reshape.84
  246.7 0.7 add_multiply_fusion
  (58 shorter events, 2.3 us)
Async XLA Ops:
  8.0 13.1 %copy-start = (bf16[4,1024,32]{1,2,0:T(8,128)(2,1)S(1)}, bf16[4,1024,32]{1,2,0:T(8,128)(2,1)}, u32[]{:S(2)}) copy-start(bf16[4,1024,32]{1,2,0:T(8,128)(2,1)} %param.12) | copy-start | bytes 786436
  8.0 1.9 copy-start.2
  9.9 1.2 copy-start.4
  11.2 0.7 copy-start.5
  13.0 2.0 copy-start.1
  15.0 84.1 %all-to-all-start = ((bf16[16,128,1024]{2,1,0:T(8,128)(2,1)}), bf16[16,128,1024]{2,1,0:T(8,128)(2,1)}, u32[]{:S(2)}, u32[]{:S(2)}) async-start(bf16[16,128,1024]{2,1,0:T(8,128)(2,1)} %copy-done.1), calls=%async_computation | async-start | bytes 8388608 | tf_op jit(solution)/shard_map/all_to_all | solution.py:244
  21.0 1.6 copy-start.6
  21.0 162.0 %all-gather.3.cloned.1.call-start = ((), (), s32[]{:S(2)}) async-start(), calls=%async_computation.7 | async-start | bytes 2162688 | tf_op jit(solution)/shard_map/all_gather | solution.py:236
  22.6 15.8 %copy-start.8 = (bf16[12,32,64]{2,1,0:T(8,128)(2,1)S(1)}, bf16[12,32,64]{2,1,0:T(8,128)(2,1)}, u32[]{:S(2)}) copy-start(bf16[12,32,64]{2,1,0:T(8,128)(2,1)} %param.13) | copy-start | bytes 147460
  24.1 27.9 %collective-permute-start = (bf16[4,32,1024]{2,1,0:T(8,128)(2,1)S(1)}, bf16[4,32,1024]{2,1,0:T(8,128)(2,1)S(1)}, u32[]{:S(2)}, u32[]{:S(2)}) collective-permute-start(bf16[4,32,1024]{2,1,0:T(8,128)(2,1)S(1)} %pad_maximum_fusion.1), channel_id=1, source_target_pairs={{0,0},{1,33},{2,66},{3,99},{4,132},{5,165},{6,198},{7,231},{8,264}... | collective-permute-start | bytes 786440 | tf_op jit(solution)/shard_map/ppermute | solution.py:222
  38.5 9.8 %collective-permute-start.3 = (bf16[48,128]{1,0:T(8,128)(2,1)S(1)}, bf16[48,128]{1,0:T(8,128)(2,1)S(1)}, u32[]{:S(2)}, u32[]{:S(2)}) collective-permute-start(bf16[48,128]{1,0:T(8,128)(2,1)S(1)} %get-tuple-element.12), channel_id=1, source_target_pairs={{0,96},{32,64},{64,32},{96,0},{128,224},{160,192},{192,160},{224,1... | collective-permute-start | bytes 36872 | tf_op jit(solution)/shard_map/ppermute | solution.py:232
  42.1 6.5 %collective-permute-start.2 = (bf16[48,128]{1,0:T(8,128)(2,1)S(1)}, bf16[48,128]{1,0:T(8,128)(2,1)S(1)}, u32[]{:S(2)}, u32[]{:S(2)}) collective-permute-start(bf16[48,128]{1,0:T(8,128)(2,1)S(1)} %get-tuple-element.13), channel_id=1, source_target_pairs={{0,64},{32,96},{64,0},{96,32},{128,192},{160,224},{192,128},{224,1... | collective-permute-start | bytes 36872 | tf_op jit(solution)/shard_map/ppermute | solution.py:232
  46.4 5.6 %collective-permute-start.1 = (bf16[48,128]{1,0:T(8,128)(2,1)S(1)}, bf16[48,128]{1,0:T(8,128)(2,1)S(1)}, u32[]{:S(2)}, u32[]{:S(2)}) collective-permute-start(bf16[48,128]{1,0:T(8,128)(2,1)S(1)} %get-tuple-element.14), channel_id=1, source_target_pairs={{0,32},{32,0},{64,96},{96,64},{128,160},{160,128},{192,224},{224,1... | collective-permute-start | bytes 36872 | tf_op jit(solution)/shard_map/ppermute | solution.py:232
  52.7 168.2 %reduce-scatter.2.cloned.1.call-start = ((), (), s32[]{:S(2)}) async-start(), calls=%async_computation.6 | async-start | bytes 2228224 | tf_op jit(solution)/shard_map/reduce_scatter | solution.py:252
  52.8 38.2 %collective-permute-start.4 = (bf16[4,48,128]{2,1,0:T(8,128)(2,1)S(1)}, bf16[4,48,128]{2,1,0:T(8,128)(2,1)S(1)}, u32[]{:S(2)}, u32[]{:S(2)}) collective-permute-start(bf16[4,48,128]{2,1,0:T(8,128)(2,1)S(1)} %pad_maximum_fusion.2), channel_id=1, source_target_pairs={{0,128},{32,160},{64,192},{96,224},{128,0},{160,32},{192,64},{224,... | collective-permute-start | bytes 147464 | tf_op jit(solution)/shard_map/ppermute | solution.py:237
  74.0 16.9 %collective-permute-start.5 = (bf16[4,48,128]{2,1,0:T(8,128)(2,1)S(1)}, bf16[4,48,128]{2,1,0:T(8,128)(2,1)S(1)}, u32[]{:S(2)}, u32[]{:S(2)}) collective-permute-start(bf16[4,48,128]{2,1,0:T(8,128)(2,1)S(1)} %pad_maximum_fusion.2), channel_id=1, source_target_pairs={{0,256},{32,288},{64,320},{96,352},{128,384},{160,416},{192,448},{... | collective-permute-start | bytes 147464 | tf_op jit(solution)/shard_map/ppermute | solution.py:237
  88.4 9.9 %collective-permute-start.6 = (bf16[4,48,128]{2,1,0:T(8,128)(2,1)S(1)}, bf16[4,48,128]{2,1,0:T(8,128)(2,1)S(1)}, u32[]{:S(2)}, u32[]{:S(2)}) collective-permute-start(bf16[4,48,128]{2,1,0:T(8,128)(2,1)S(1)} %pad_maximum_fusion.2), channel_id=1, source_target_pairs={{0,384},{32,416},{64,448},{96,480},{128,256},{160,288},{192,320},{... | collective-permute-start | bytes 147464 | tf_op jit(solution)/shard_map/ppermute | solution.py:237
  108.9 65.4 %all-to-all-start.1 = ((bf16[8,3,64,512]{3,2,1,0:T(8,128)(2,1)}), bf16[8,3,64,512]{3,2,1,0:T(8,128)(2,1)S(1)}, u32[]{:S(2)}, u32[]{:S(2)}) async-start(bf16[8,3,64,512]{3,2,1,0:T(8,128)(2,1)} %broadcast_in_dim.7), calls=%async_computation.2 | async-start | bytes 3145728 | tf_op jit(solution)/shard_map/all_to_all | solution.py:185
  129.3 26.4 %collective-permute-start.10 = (bf16[3,32,1024]{2,1,0:T(8,128)(2,1)S(1)}, bf16[3,32,1024]{2,1,0:T(8,128)(2,1)S(1)}, u32[]{:S(2)}, u32[]{:S(2)}) collective-permute-start(bf16[3,32,1024]{2,1,0:T(8,128)(2,1)S(1)} %slice.6), channel_id=1, source_target_pairs={{0,12},{4,8},{8,4},{12,0},{1,13},{5,9},{9,5},{13,1},{2,14},{6,10},... | collective-permute-start | bytes 589832 | tf_op jit(solution)/shard_map/ppermute | solution.py:248
  131.2 43.1 %collective-permute-start.9 = (bf16[3,32,1024]{2,1,0:T(8,128)(2,1)S(1)}, bf16[3,32,1024]{2,1,0:T(8,128)(2,1)S(1)}, u32[]{:S(2)}, u32[]{:S(2)}) collective-permute-start(bf16[3,32,1024]{2,1,0:T(8,128)(2,1)S(1)} %slice.6), channel_id=1, source_target_pairs={{0,8},{4,12},{8,0},{12,4},{1,9},{5,13},{9,1},{13,5},{2,10},{6,14},... | collective-permute-start | bytes 589832 | tf_op jit(solution)/shard_map/ppermute | solution.py:248
  146.0 28.2 %collective-permute-start.8 = (bf16[3,32,1024]{2,1,0:T(8,128)(2,1)S(1)}, bf16[3,32,1024]{2,1,0:T(8,128)(2,1)S(1)}, u32[]{:S(2)}, u32[]{:S(2)}) collective-permute-start(bf16[3,32,1024]{2,1,0:T(8,128)(2,1)S(1)} %slice.6), channel_id=1, source_target_pairs={{0,4},{4,0},{8,12},{12,8},{1,5},{5,1},{9,13},{13,9},{2,6},{6,2},{1... | collective-permute-start | bytes 589832 | tf_op jit(solution)/shard_map/ppermute | solution.py:248
  175.6 12.1 %all-to-all-start.2 = ((bf16[8,3,32,128]{3,2,1,0:T(8,128)(2,1)}), bf16[8,3,32,128]{3,2,1,0:T(8,128)(2,1)S(1)}, u32[]{:S(2)}, u32[]{:S(2)}) async-start(bf16[8,3,32,128]{3,2,1,0:T(8,128)(2,1)} %shard_map.97), calls=%async_computation.3 | async-start | bytes 393216 | tf_op jit(solution)/shard_map/all_to_all | solution.py:268
  187.7 1.6 copy-start.3
  216.7 27.3 %collective-permute-start.11 = (bf16[3,32,1024]{2,1,0:T(8,128)(2,1)S(1)}, bf16[3,32,1024]{2,1,0:T(8,128)(2,1)S(1)}, u32[]{:S(2)}, u32[]{:S(2)}) collective-permute-start(bf16[3,32,1024]{2,1,0:T(8,128)(2,1)S(1)} %reduce_sum.12), channel_id=1, source_target_pairs={{0,0},{33,1},{66,2},{99,3},{132,4},{165,5},{198,6},{231,7},{264,8}... | collective-permute-start | bytes 589832 | tf_op jit(solution)/shard_map/ppermute | solution.py:276
  220.8 25.9 %copy-start.7 = (bf16[64,1024]{1,0:T(8,128)(2,1)S(1)}, bf16[64,1024]{1,0:T(8,128)(2,1)}, u32[]{:S(2)}) copy-start(bf16[64,1024]{1,0:T(8,128)(2,1)} %reduce-scatter.2.cloned.1.call-done) | copy-start | bytes 393220
  221.8 25.0 %collective-permute-start.7 = (bf16[1,32,1024]{2,1,0:T(8,128)(2,1)S(1)}, bf16[1,32,1024]{2,1,0:T(8,128)(2,1)S(1)}, u32[]{:S(2)}, u32[]{:S(2)}) collective-permute-start(bf16[1,32,1024]{2,1,0:T(8,128)(2,1)S(1)} %constant_dynamic-slice_fusion), channel_id=1, source_target_pairs={{0,16},{16,0},{1,17},{17,1},{2,18},{18,2},{3,19},{19,3},{4,20},{20... | collective-permute-start | bytes 196616 | tf_op jit(solution)/shard_map/ppermute | solution.py:257
Sparse Core Ops, SparseCore 0:
  52.8 119.7 all-gather.2
Sparse Core Ops, SparseCore 1:
  107.5 93.2 reduce-scatter.1
